TPU v7x, 32 devices: a whole 2x2x4 slice. The times are simulated.
32 devices in a mesh: stratum: 8 (over z, core), replica: 4 (over y, x).
Axes of the slice: x: 2, y: 2, z: 4, core: 2. Of those that a mesh axis runs over, the one named last changes fastest.
Arguments:
- user_factors: float32 [131072, 128], P(('stratum', 'replica')), may hold values from -1.8 to 1.8
- item_factors: float32 [32768, 128], P('stratum'), may hold values from -1.8 to 1.8
- ratings: bfloat16 [2, 8192, 128, 128], P(None, ('stratum', 'replica')), may hold values from -9 to 9
- user_tile: int32 [2, 8192], P(None, ('stratum', 'replica')), may hold values from 0 to 31, as said below
- item_tile: int32 [2, 8192], P(None, ('stratum', 'replica')), may hold values from 0 to 31, as said below
- live_count: int32 [2, 32], P(None, ('stratum', 'replica')), may hold values from 64 to 256, as said below
- partner: int32 [8], replicated, may hold values from 0 to 7, as said below
Outputs:
- user_out: float32 [131072, 128], P(('stratum', 'replica'))
- item_out: float32 [32768, 128], P('stratum')
Inputs may be any that keep to these rules, and one draw needn't show every extreme that they name: partner[i] = i XOR m for one m from 4 to 7, the same for every i. `user_tile`: within one device and one sub-epoch, its 256 slots name distinct pairs of user tile and item tile. `item_tile`: paired with user_tile as stated there. `live_count`: in every sub-epoch some device has all 256 slots live.
All inputs are finite; a program needn't handle non-finite values.
Results may differ from a plain program's by a relative error of at most 0.0012.
Values sent between devices are 32-bit elements; how exact they have to be, the bound alone decides.
No kernel may reach another device: no remote copies, remote signals or barrier semaphores. Data moves between devices by JAX's collectives and lax.ppermute only.
A program may use at most 128 MiB of HBM per device.

v0:
```python
import functools

import jax
import jax.numpy as jnp
from jax import lax
from jax.experimental import pallas as pl
from jax.experimental.pallas import tpu as pltpu
from jax.sharding import PartitionSpec as P

LEARNING_RATE = 0.05
WEIGHT_DECAY = 0.05
KEEP = 1.0 - LEARNING_RATE * WEIGHT_DECAY

TILE = 128
CHUNKS = 2
UNITS = 8
AHEAD = 4
RING = AHEAD + 1
FIELD = 6
COUNT_ROWS = 8
VMEM_BYTES = 24 << 20
SLOT_VMEM_BYTES = 44 << 20

CONTRACT_LAST = (((1,), (1,)), ((), ()))
VMEM = pl.BlockSpec(memory_space=pltpu.VMEM)
SMEM = pl.BlockSpec(memory_space=pltpu.SMEM)
ANY = pl.BlockSpec(memory_space=pl.ANY)
PARAMS = pltpu.CompilerParams(vmem_limit_bytes=VMEM_BYTES)


def up(value, unit):
    return (value + unit - 1) // unit * unit


class Layout:
    def __init__(self, users, items, slots, chunks, replicas):
        self.users, self.items, self.slots = users, items, slots
        self.chunks, self.replicas = chunks, replicas
        self.tiles = items // chunks
        self.share = self.tiles // replicas
        self.groups = chunks * users
        self.cap = slots + self.groups
        self.step = 2 * UNITS
        self.order_cols = up(self.cap, 128)
        self.group_cols = up(self.groups + 1, 128)
        self.item_cols = up(items, 128)
        self.base_at = self.order_cols
        self.count_at = self.base_at + self.group_cols
        self.seen_at = self.count_at + self.group_cols
        self.columns = self.seen_at + self.item_cols


def column(row, across):
    return jnp.broadcast_to(row, (across, row.shape[1])).T


def low_tiles(rows, low_ref, lowt_ref, a):
    low_ref[a] = rows.astype(jnp.bfloat16)
    lowt_ref[a] = rows.T.astype(jnp.bfloat16)


def prepare_kernel(lay, epochs, user_ref, item_ref, live_ref, rows_ref, table_ref, low_ref, lowt_ref):
    def iota(shape, axis):
        return lax.broadcasted_iota(jnp.int32, shape, axis)

    def total(mask, values=1):
        return jnp.sum(jnp.where(mask, values, 0), axis=0, keepdims=True)

    n, groups = lay.slots, lay.group_cols
    for e in range(epochs):
        user, item = user_ref[e : e + 1, :], item_ref[e : e + 1, :]
        live = iota((1, n), 1) < live_ref[e : e + 1, :]
        group = jnp.where(live, item // lay.tiles * lay.users + user, lay.groups)
        packed = user + (item << FIELD) + (iota((1, n), 1) << 2 * FIELD)
        same = column(group, n) == group
        rank = total(same & (iota((n, n), 0) < iota((n, n), 1)))
        count = total(column(group, groups) == iota((n, groups), 1))
        padded = (count + 1) // 2 * 2
        base = total(iota((groups, groups), 0) < iota((groups, groups), 1), column(padded, groups))
        place = rank + total(iota((groups, n), 0) == group, column(base, n))
        place = jnp.where(live, place, -1)
        order = total(column(place, lay.order_cols) == iota((n, lay.order_cols), 1), column(packed, lay.order_cols))
        every = iota((1, groups), 1)
        spare = jnp.where((count % 2 == 1) & (every < lay.groups), base + count, -1)
        order += total(
            column(spare, lay.order_cols) == iota((groups, lay.order_cols), 1),
            column(every % lay.users + (lay.items << FIELD), lay.order_cols),
        )
        tile = jnp.where(live, item, lay.items)
        seen = total(column(tile, lay.item_cols) == iota((n, lay.item_cols), 1))
        table_ref[e : e + 1, 0 : lay.base_at] = order
        table_ref[e : e + 1, lay.base_at : lay.count_at] = base
        table_ref[e : e + 1, lay.count_at : lay.seen_at] = count
        table_ref[e : e + 1, lay.seen_at : lay.columns] = seen

    def lower(a, _):
        low_tiles(rows_ref[pl.ds(pl.multiple_of(a * TILE, TILE), TILE), :], low_ref, lowt_ref, a)
        return 0

    lax.fori_loop(0, lay.users, lower, 0, unroll=4)
    low_ref[lay.users] = jnp.zeros((TILE, TILE), jnp.bfloat16)
    lowt_ref[lay.users] = jnp.zeros((TILE, TILE), jnp.bfloat16)


def low_shape(lay):
    return jax.ShapeDtypeStruct((lay.users + 1, TILE, TILE), jnp.bfloat16)


def prepare(lay, user_tile, item_tile, live_count, user_rows):
    epochs = user_tile.shape[0]
    return pl.pallas_call(
        functools.partial(prepare_kernel, lay, epochs),
        out_shape=[jax.ShapeDtypeStruct((epochs, lay.columns), jnp.int32), low_shape(lay), low_shape(lay)],
        in_specs=[VMEM] * 4,
        out_specs=[VMEM] * 3,
        compiler_params=PARAMS,
        name="prepare",
    )(user_tile, item_tile, live_count, user_rows)


def slots_kernel(lay, epoch, chunk, pieces_in, table_ref, me_ref, ratings_ref, low_ref, lowt_ref, *refs):
    block_refs, refs = refs[:pieces_in], refs[pieces_in:]
    user_grad, piece_refs = refs[0], refs[1 : 1 + lay.replicas]
    buf, sems, item_low, item_grad = refs[1 + lay.replicas :]
    me = me_ref[0]
    begin = table_ref[epoch, lay.base_at + chunk * lay.users]
    end = table_ref[epoch, lay.base_at + (chunk + 1) * lay.users]
    steps = (end - begin + lay.step - 1) // lay.step
    zero = jnp.zeros((TILE, TILE), jnp.float32)

    def fetch(g):
        for s in range(lay.step):
            packed = table_ref[epoch, jnp.minimum(begin + g * lay.step + s, lay.cap - 1)]
            slot = lax.shift_right_logical(packed, 2 * FIELD)
            pltpu.make_async_copy(ratings_ref.at[epoch, slot], buf.at[g % RING, s], sems.at[g % RING]).start()

    def fetch_first(g, _):
        fetch(g)
        return 0

    lax.fori_loop(0, jnp.minimum(AHEAD, steps), fetch_first, 0)

    for j in range(lay.tiles):
        item_grad[j] = zero
    if pieces_in == 1:
        for j in range(lay.tiles):
            item_low[j] = block_refs[0][j * TILE : (j + 1) * TILE, :].astype(jnp.bfloat16)
    else:
        for k in range(lay.replicas):
            first = lax.bitwise_xor(me, k) * lay.share
            for j in range(lay.share):
                item_low[first + j] = block_refs[k][j * TILE : (j + 1) * TILE, :].astype(jnp.bfloat16)
    item_low[lay.tiles] = jnp.zeros((TILE, TILE), jnp.bfloat16)

    def clear(a, _):
        user_grad[a] = zero
        return 0

    lax.fori_loop(0, lay.users, clear, 0, unroll=4)

    def step(g, _):
        @pl.when(g + AHEAD < steps)
        def _():
            fetch(g + AHEAD)

        first = begin + g * lay.step
        here = buf.at[g % RING]
        pltpu.make_async_copy(ratings_ref.at[epoch, pl.ds(0, lay.step)], here, sems.at[g % RING]).wait()
        units = []
        for n in range(UNITS):
            items = []
            for s in range(2):
                place = first + 2 * n + s
                packed = table_ref[epoch, jnp.minimum(place, lay.cap - 1)]
                item = lax.shift_right_logical(packed, FIELD) % (1 << FIELD) - chunk * lay.tiles
                items.append(jnp.where((place < end) & (item >= 0) & (item < lay.tiles), item, lay.tiles))
            user = jnp.where(place < end, packed % (1 << FIELD), lay.users)
            right = jnp.concatenate([item_low[b] for b in items], axis=0)
            predicted = lax.dot_general(low_ref[user], right, CONTRACT_LAST, preferred_element_type=jnp.float32)
            rating = jnp.concatenate([buf[g % RING, 2 * n + s] for s in range(2)], axis=1)
            residual = (rating.astype(jnp.float32) - predicted).astype(jnp.bfloat16)
            units.append((user, items, right, residual))
        for user, items, right, residual in units:
            user_grad[user] += jnp.dot(residual, right, preferred_element_type=jnp.float32)
            part = jnp.dot(lowt_ref[user], residual, preferred_element_type=jnp.float32)
            for s in range(2):
                item_grad[items[s]] += part[:, s * TILE : (s + 1) * TILE]
        return 0

    lax.fori_loop(0, steps, step, 0)

    row = lax.broadcasted_iota(jnp.int32, (COUNT_ROWS, TILE), 0)
    for k in range(lay.replicas):
        first = lax.bitwise_xor(me, k) * lay.share
        counts = jnp.zeros((COUNT_ROWS, TILE), jnp.int32)
        for j in range(lay.share):
            piece_refs[k][j * TILE : (j + 1) * TILE, :] = item_grad[first + j].T
            seen = table_ref[epoch, lay.seen_at + chunk * lay.tiles + first + j]
            counts = jnp.where(row == j, seen, counts)
        piece_refs[k][lay.share * TILE :, :] = counts.astype(jnp.float32)


def slot_terms(lay, epoch, chunk, table, me, ratings, low, lowt, blocks):
    if len(blocks) == 1:
        block_specs = [pl.BlockSpec((lay.tiles * TILE, TILE), lambda i: (chunk, 0))]
    else:
        block_specs = [VMEM] * len(blocks)
    piece = jax.ShapeDtypeStruct((lay.share * TILE + COUNT_ROWS, TILE), jnp.float32)
    user_grad = jax.ShapeDtypeStruct((lay.users + 1, TILE, TILE), jnp.float32)
    live = lay.slots // lay.chunks
    out = pl.pallas_call(
        functools.partial(slots_kernel, lay, epoch, chunk, len(blocks)),
        grid=(1,),
        out_shape=[user_grad] + [piece] * lay.replicas,
        in_specs=[SMEM, SMEM, ANY, VMEM, VMEM] + block_specs,
        out_specs=[VMEM] * (1 + lay.replicas),
        scratch_shapes=[
            pltpu.VMEM((RING, lay.step, TILE, TILE), jnp.bfloat16),
            pltpu.SemaphoreType.DMA((RING,)),
            pltpu.VMEM((lay.tiles + 1, TILE, TILE), jnp.bfloat16),
            pltpu.VMEM((lay.tiles + 1, TILE, TILE), jnp.float32),
        ],
        cost_estimate=pl.CostEstimate(
            flops=6 * live * TILE**3 * 4, bytes_accessed=live * TILE * TILE * 2, transcendentals=0
        ),
        compiler_params=pltpu.CompilerParams(vmem_limit_bytes=SLOT_VMEM_BYTES),
        name="slots",
    )(table, me, ratings, low, lowt, *blocks)
    return out[0], list(out[1:])


def user_kernel(lay, epoch, last, table_ref, rows_ref, *refs):
    grads, refs = refs[: lay.chunks], refs[lay.chunks :]

    def one(a, _):
        seen = sum(table_ref[epoch, lay.count_at + c * lay.users + a] for c in range(lay.chunks))
        seen = jnp.maximum(jnp.broadcast_to(seen, (1, TILE)).astype(jnp.float32), 1.0)
        at = pl.ds(pl.multiple_of(a * TILE, TILE), TILE)
        grad = sum(grad_ref[a] for grad_ref in grads)
        rows = rows_ref[at, :] * KEEP + grad * (LEARNING_RATE / seen)
        refs[0][at, :] = rows
        if not last:
            low_tiles(rows, refs[1], refs[2], a)
        return 0

    lax.fori_loop(0, lay.users, one, 0, unroll=4)
    if not last:
        refs[1][lay.users] = jnp.zeros((TILE, TILE), jnp.bfloat16)
        refs[2][lay.users] = jnp.zeros((TILE, TILE), jnp.bfloat16)


def user_step(lay, epoch, last, table, rows, grads):
    out_shape = [jax.ShapeDtypeStruct(rows.shape, jnp.float32)]
    if not last:
        out_shape += [low_shape(lay)] * 2
    return pl.pallas_call(
        functools.partial(user_kernel, lay, epoch, last),
        out_shape=out_shape,
        in_specs=[SMEM] + [VMEM] * (1 + len(grads)),
        out_specs=[VMEM] * len(out_shape),
        compiler_params=PARAMS,
        name="users",
    )(table, rows, *grads)


def item_kernel(lay, me_ref, old_ref, *refs):
    parts, out_ref = refs[:-1], refs[-1]
    for j in range(lay.share):
        at = slice(j * TILE, (j + 1) * TILE)
        row = lay.share * TILE + j
        seen = jnp.maximum(sum(part[row : row + 1, :] for part in parts), 1.0)
        grad = sum(part[at, :] for part in parts)
        out_ref[at, :] = old_ref[at, :] * KEEP + grad * (LEARNING_RATE / seen)


def item_step(lay, chunk, me, old, parts):
    rows = lay.share * TILE
    whole = old.shape[0] != rows
    grid_spec = pltpu.PrefetchScalarGridSpec(
        num_scalar_prefetch=1,
        grid=(1,),
        in_specs=[
            pl.BlockSpec((rows, TILE), lambda i, me: (chunk * lay.replicas + me[0] if whole else 0, 0))
        ]
        + [VMEM] * len(parts),
        out_specs=pl.BlockSpec((rows, TILE), lambda i, me: (0, 0)),
    )
    return pl.pallas_call(
        functools.partial(item_kernel, lay),
        grid_spec=grid_spec,
        out_shape=jax.ShapeDtypeStruct((rows, TILE), jnp.float32),
        compiler_params=PARAMS,
        name="items",
    )(me, old, *parts)


def assemble_kernel(lay, me_ref, *refs):
    pieces, out_ref, sems = refs[:-2], refs[-2], refs[-1]
    rows = lay.share * TILE
    copies = []
    for c in range(lay.chunks):
        for k in range(lay.replicas):
            first = (c * lay.replicas + lax.bitwise_xor(me_ref[0], k)) * rows
            at = pl.ds(pl.multiple_of(first, TILE), rows)
            n = c * lay.replicas + k
            copies.append(pltpu.make_async_copy(pieces[n], out_ref.at[at, :], sems.at[n]))
            copies[-1].start()
    for copy in copies:
        copy.wait()


def assemble(lay, me, pieces):
    return pl.pallas_call(
        functools.partial(assemble_kernel, lay),
        out_shape=jax.ShapeDtypeStruct((lay.items * TILE, TILE), jnp.float32),
        in_specs=[SMEM] + [VMEM] * len(pieces),
        out_specs=ANY,
        scratch_shapes=[pltpu.SemaphoreType.DMA((len(pieces),))],
        compiler_params=PARAMS,
        name="assemble",
    )(me, *pieces)


def swap(value, axis, mask):
    return lax.ppermute(value, axis, [(i, i ^ mask) for i in range(lax.axis_size(axis))])


def gather_sum(pieces, bits):
    held = {k: [piece] for k, piece in enumerate(pieces)}
    for bit in bits:
        for k in [k for k in held if k & bit]:
            sent = held.pop(k)
            held[k ^ bit] = held[k ^ bit] + [swap(functools.reduce(jnp.add, sent), "replica", bit)]
    return held[0]


def spread(own, bits):
    held = {0: own}
    for bit in reversed(bits):
        for k in list(held):
            held[k ^ bit] = swap(held[k], "replica", bit)
    return [held[k] for k in sorted(held)]


def steps(flip, lay, user_factors, item_factors, ratings, user_tile, item_tile, live_count):
    me = lax.axis_index("replica").astype(jnp.int32).reshape(1)
    levels = lay.replicas.bit_length() - 1
    bits = [[1 << (c + i) % levels for i in range(levels)] for c in range(lay.chunks)]
    epochs = ratings.shape[0]
    rows = user_factors
    table, low, lowt = prepare(lay, user_tile, item_tile, live_count, rows)
    blocks = [[item_factors]] * lay.chunks
    for e in range(epochs):
        last = e + 1 == epochs
        grads, parts = [], []
        for c in range(lay.chunks):
            grad, pieces = slot_terms(lay, e, c, table, me, ratings, low, lowt, blocks[c])
            grads.append(grad)
            parts.append(gather_sum(pieces, bits[c]))
        if last:
            (rows,) = user_step(lay, e, last, table, rows, grads)
        else:
            rows, low, lowt = user_step(lay, e, last, table, rows, grads)
        fresh = []
        for c in range(lay.chunks):
            own = item_step(lay, c, me, blocks[c][0], parts[c])
            if not last:
                own = swap(own, "stratum", flip)
            fresh.append(spread(own, bits[c]))
        blocks = fresh
    return rows, assemble(lay, me, [piece for chunk in blocks for piece in chunk])


def local(user_factors, item_factors, ratings, user_tile, item_tile, live_count, partner):
    users, items = user_factors.shape[0] // TILE, item_factors.shape[0] // TILE
    replicas, strata = lax.axis_size("replica"), lax.axis_size("stratum")
    lay = Layout(users, items, ratings.shape[1], CHUNKS, replicas)
    branches = [functools.partial(steps, flip, lay) for flip in range(strata // 2, strata)]
    args = (user_factors, item_factors, ratings, user_tile, item_tile, live_count)
    return lax.switch(partner[0] - strata // 2, branches, *args)


def solution(mesh):
    split = P(("stratum", "replica"), None)
    return jax.shard_map(
        local,
        mesh=mesh,
        in_specs=(
            split,
            P("stratum", None),
            P(None, ("stratum", "replica"), None, None),
            P(None, ("stratum", "replica")),
            P(None, ("stratum", "replica")),
            P(None, ("stratum", "replica")),
            P(),
        ),
        out_specs=(split, P("stratum", None)),
        check_vma=False,
    )
```

profile of v0, /device:TPU:20, one launch (start us, length us, event | category | flops | bytes accessed | tf_op | source)
XLA Modules:
  0.0 132.9 jit_solution(9889854121742913701)
XLA Ops:
  1.3 131.4 %conditional.1 = (f32[4096,128]{1,0:T(8,128)}, f32[4096,128]{1,0:T(8,128)}) conditional(s32[]{:T(128)} %bitcast.4, (s32[2,256]{1,0:T(2,128)}, s32[2,256]{1,0:T(2,128)}, s32[2,1]{0,1:T(1,128)}, f32[4096,128]{1,0:T(8,128)}, bf16[2,256,128,128]{3,2,1,0:T(8,128)(2,1)}, /*index=5*/f32[4096,128]{1,0:T(8,128)}) %tuple.23, ...), branch_computations={%region_0.0_spmd, %region_1.0_spmd, %region_2.0_spmd, %region_3.0_... | conditional | flops 25770065920 | bytes 72598680 | solution.py:380
  2.2 3.1 %prepare.5 = (s32[2,768]{1,0:T(2,128)S(1)}, bf16[33,128,128]{2,1,0:T(8,128)(2,1)S(1)}, bf16[33,128,128]{2,1,0:T(8,128)(2,1)S(1)}) custom-call(s32[2,256]{1,0:T(2,128)} %get-tuple-element.80.user_ref, s32[2,256]{1,0:T(2,128)} %get-tuple-element.81.item_ref, s32[2,1]{1,0:T(2,128)S(1)} %copy.18.live_ref, f32[4096,128]{1,0:T(8,128)} %get-tuple-element.83.rows_ref), custom_call_target="tpu_custom_call" | custom-call | tf_op jit(solution)/shard_map/cond/branch_1_fun/prepare/pallas_call | solution.py:111
  5.3 6.1 %slots.20 = (f32[33,128,128]{2,1,0:T(8,128)S(1)}, f32[520,128]{1,0:T(8,128)S(1)}, f32[520,128]{1,0:T(8,128)S(1)}, f32[520,128]{1,0:T(8,128)S(1)}, f32[520,128]{1,0:T(8,128)S(1)}) custom-call(s32[2,768]{1,0:T(2,128)S(1)} %get-tuple-element.84.table_ref, s32[1]{0:T(128)} %bitcast.1.me_ref, bf16[2,256,128,128]{3,2,1,0:T(8,128)(2,1)} %get-tuple-element.85.ratings_ref, ...), custom_call_target="tpu_custom_call" | custom-call | flops 6442450944 | bytes 4194304 | tf_op jit(solution)/shard_map/cond/branch_1_fun/slots/pallas_call | solution.py:211
  13.1 6.3 %slots.21 = (f32[33,128,128]{2,1,0:T(8,128)S(1)}, f32[520,128]{1,0:T(8,128)S(1)}, f32[520,128]{1,0:T(8,128)S(1)}, f32[520,128]{1,0:T(8,128)S(1)}, f32[520,128]{1,0:T(8,128)S(1)}) custom-call(s32[2,768]{1,0:T(2,128)S(1)} %get-tuple-element.84.table_ref, s32[1]{0:T(128)} %bitcast.1.me_ref, bf16[2,256,128,128]{3,2,1,0:T(8,128)(2,1)} %get-tuple-element.85.ratings_ref, ...), custom_call_target="tpu_custom_call" | custom-call | flops 6442450944 | bytes 4194304 | tf_op jit(solution)/shard_map/cond/branch_1_fun/slots/pallas_call | solution.py:211
  22.1 4.9 %collective-permute-done.34 = f32[520,128]{1,0:T(8,128)S(1)} collective-permute-done((f32[520,128]{1,0:T(8,128)S(1)}, f32[520,128]{1,0:T(8,128)S(1)}, u32[]{:S(2)}, u32[]{:S(2)}) %collective-permute-start.34) | collective-permute-done | bytes 266272 | tf_op jit(solution)/shard_map/cond/branch_1_fun/ppermute | solution.py:325
  27.2 5.6 %collective-permute-done.28.refs_2_ = f32[520,128]{1,0:T(8,128)S(1)} collective-permute-done((f32[520,128]{1,0:T(8,128)S(1)}, f32[520,128]{1,0:T(8,128)S(1)}, u32[]{:S(2)}, u32[]{:S(2)}) %collective-permute-start.28) | collective-permute-done | bytes 266272 | tf_op jit(solution)/shard_map/cond/branch_1_fun/ppermute | solution.py:325
  32.9 5.5 %collective-permute-done.33.refs_1_ = f32[520,128]{1,0:T(8,128)S(1)} collective-permute-done((f32[520,128]{1,0:T(8,128)S(1)}, f32[520,128]{1,0:T(8,128)S(1)}, u32[]{:S(2)}, u32[]{:S(2)}) %collective-permute-start.33) | collective-permute-done | bytes 266272 | tf_op jit(solution)/shard_map/cond/branch_1_fun/ppermute | solution.py:325
  39.7 15.8 %collective-permute-done.36.refs_0_.old_ref = f32[512,128]{1,0:T(8,128)S(1)} collective-permute-done((f32[512,128]{1,0:T(8,128)S(1)}, f32[512,128]{1,0:T(8,128)S(1)}, u32[]{:S(2)}, u32[]{:S(2)}) %collective-permute-start.36) | collective-permute-done | bytes 262176 | tf_op jit(solution)/shard_map/cond/branch_1_fun/ppermute | solution.py:325
  55.6 2.0 %collective-permute-start.30 = (f32[512,128]{1,0:T(8,128)S(1)}, f32[512,128]{1,0:T(8,128)S(1)}, u32[]{:S(2)}, u32[]{:S(2)}) collective-permute-start(f32[512,128]{1,0:T(8,128)S(1)} %collective-permute-done.29.refs_0_.old_ref), channel_id=1, source_target_pairs={{0,1},{1,0},{2,3},{3,2},{4,5},{5,4},{6,7},{7,6},{8,9},{9,8},{10,11... | collective-permute-start | bytes 786440 | tf_op jit(solution)/shard_map/cond/branch_1_fun/ppermute | solution.py:325
  60.0 4.0 %collective-permute-done.37.refs_1_ = f32[512,128]{1,0:T(8,128)S(1)} collective-permute-done((f32[512,128]{1,0:T(8,128)S(1)}, f32[512,128]{1,0:T(8,128)S(1)}, u32[]{:S(2)}, u32[]{:S(2)}) %collective-permute-start.37) | collective-permute-done | bytes 262176 | tf_op jit(solution)/shard_map/cond/branch_1_fun/ppermute | solution.py:325
  64.6 5.0 %collective-permute-done.30.refs_1_ = f32[512,128]{1,0:T(8,128)S(1)} collective-permute-done((f32[512,128]{1,0:T(8,128)S(1)}, f32[512,128]{1,0:T(8,128)S(1)}, u32[]{:S(2)}, u32[]{:S(2)}) %collective-permute-start.30) | collective-permute-done | bytes 262176 | tf_op jit(solution)/shard_map/cond/branch_1_fun/ppermute | solution.py:325
  69.6 5.6 %collective-permute-done.32.refs_3_ = f32[512,128]{1,0:T(8,128)S(1)} collective-permute-done((f32[512,128]{1,0:T(8,128)S(1)}, f32[512,128]{1,0:T(8,128)S(1)}, u32[]{:S(2)}, u32[]{:S(2)}) %collective-permute-start.32) | collective-permute-done | bytes 262176 | tf_op jit(solution)/shard_map/cond/branch_1_fun/ppermute | solution.py:325
  75.2 6.2 %slots.22 = (f32[33,128,128]{2,1,0:T(8,128)S(1)}, f32[520,128]{1,0:T(8,128)S(1)}, f32[520,128]{1,0:T(8,128)S(1)}, f32[520,128]{1,0:T(8,128)S(1)}, f32[520,128]{1,0:T(8,128)S(1)}) custom-call(s32[2,768]{1,0:T(2,128)S(1)} %get-tuple-element.84.table_ref, s32[1]{0:T(128)} %bitcast.1.me_ref, bf16[2,256,128,128]{3,2,1,0:T(8,128)(2,1)} %get-tuple-element.85.ratings_ref, ...), custom_call_target="tpu_custom_call" | custom-call | flops 6442450944 | bytes 4194304 | tf_op jit(solution)/shard_map/cond/branch_1_fun/slots/pallas_call | solution.py:211
  83.3 6.2 %slots.23 = (f32[33,128,128]{2,1,0:T(8,128)S(1)}, f32[520,128]{1,0:T(8,128)S(1)}, f32[520,128]{1,0:T(8,128)S(1)}, f32[520,128]{1,0:T(8,128)S(1)}, f32[520,128]{1,0:T(8,128)S(1)}) custom-call(s32[2,768]{1,0:T(2,128)S(1)} %get-tuple-element.84.table_ref, s32[1]{0:T(128)} %bitcast.1.me_ref, bf16[2,256,128,128]{3,2,1,0:T(8,128)(2,1)} %get-tuple-element.85.ratings_ref, ...), custom_call_target="tpu_custom_call" | custom-call | flops 6442450944 | bytes 4194304 | tf_op jit(solution)/shard_map/cond/branch_1_fun/slots/pallas_call | solution.py:211
  89.8 3.6 %collective-permute-start.40 = (f32[520,128]{1,0:T(8,128)S(1)}, f32[520,128]{1,0:T(8,128)S(1)}, u32[]{:S(2)}, u32[]{:S(2)}) collective-permute-start(f32[520,128]{1,0:T(8,128)S(1)} %get-tuple-element.105), channel_id=1, source_target_pairs={{0,1},{1,0},{2,3},{3,2},{4,5},{5,4},{6,7},{7,6},{8,9},{9,8},{10,11... | collective-permute-start | bytes 798728 | tf_op jit(solution)/shard_map/cond/branch_1_fun/ppermute | solution.py:325
  95.6 2.5 %collective-permute-done.47 = f32[520,128]{1,0:T(8,128)S(1)} collective-permute-done((f32[520,128]{1,0:T(8,128)S(1)}, f32[520,128]{1,0:T(8,128)S(1)}, u32[]{:S(2)}, u32[]{:S(2)}) %collective-permute-start.47) | collective-permute-done | bytes 266272 | tf_op jit(solution)/shard_map/cond/branch_1_fun/ppermute | solution.py:325
  98.0 3.4 %collective-permute-start.48 = (f32[520,128]{1,0:T(8,128)S(1)}, f32[520,128]{1,0:T(8,128)S(1)}, u32[]{:S(2)}, u32[]{:S(2)}) collective-permute-start(f32[520,128]{1,0:T(8,128)S(1)} %add.41), channel_id=1, source_target_pairs={{0,1},{1,0},{2,3},{3,2},{4,5},{5,4},{6,7},{7,6},{8,9},{9,8},{10,11... | collective-permute-start | bytes 798728 | tf_op jit(solution)/shard_map/cond/branch_1_fun/ppermute | solution.py:325
  101.4 2.3 %collective-permute-done.42.refs_2_ = f32[520,128]{1,0:T(8,128)S(1)} collective-permute-done((f32[520,128]{1,0:T(8,128)S(1)}, f32[520,128]{1,0:T(8,128)S(1)}, u32[]{:S(2)}, u32[]{:S(2)}) %collective-permute-start.42) | collective-permute-done | bytes 266272 | tf_op jit(solution)/shard_map/cond/branch_1_fun/ppermute | solution.py:325
  104.2 5.2 %collective-permute-done.46.refs_1_ = f32[520,128]{1,0:T(8,128)S(1)} collective-permute-done((f32[520,128]{1,0:T(8,128)S(1)}, f32[520,128]{1,0:T(8,128)S(1)}, u32[]{:S(2)}, u32[]{:S(2)}) %collective-permute-start.46) | collective-permute-done | bytes 266272 | tf_op jit(solution)/shard_map/cond/branch_1_fun/ppermute | solution.py:325
  109.5 3.4 %collective-permute-start.49 = (f32[512,128]{1,0:T(8,128)S(1)}, f32[512,128]{1,0:T(8,128)S(1)}, u32[]{:S(2)}, u32[]{:S(2)}) collective-permute-start(f32[512,128]{1,0:T(8,128)S(1)} %items.23.refs_4_), channel_id=1, source_target_pairs={{0,1},{1,0},{2,3},{3,2},{4,5},{5,4},{6,7},{7,6},{8,9},{9,8},{10,11... | collective-permute-start | bytes 786440 | tf_op jit(solution)/shard_map/cond/branch_1_fun/ppermute | solution.py:325
  115.0 2.4 %collective-permute-start.45 = (f32[512,128]{1,0:T(8,128)S(1)}, f32[512,128]{1,0:T(8,128)S(1)}, u32[]{:S(2)}, u32[]{:S(2)}) collective-permute-start(f32[512,128]{1,0:T(8,128)S(1)} %collective-permute-done.44.refs_2_), channel_id=1, source_target_pairs={{0,1},{1,0},{2,3},{3,2},{4,5},{5,4},{6,7},{7,6},{8,9},{9,8},{10,11... | collective-permute-start | bytes 786440 | tf_op jit(solution)/shard_map/cond/branch_1_fun/ppermute | solution.py:325
  117.4 2.6 %collective-permute-done.49.refs_5_ = f32[512,128]{1,0:T(8,128)S(1)} collective-permute-done((f32[512,128]{1,0:T(8,128)S(1)}, f32[512,128]{1,0:T(8,128)S(1)}, u32[]{:S(2)}, u32[]{:S(2)}) %collective-permute-start.49) | collective-permute-done | bytes 262176 | tf_op jit(solution)/shard_map/cond/branch_1_fun/ppermute | solution.py:325
  121.5 2.4 %users.11 = f32[4096,128]{1,0:T(8,128)} custom-call(s32[2,768]{1,0:T(2,128)S(1)} %get-tuple-element.84.table_ref, f32[4096,128]{1,0:T(8,128)S(1)} %get-tuple-element.91.rows_ref, f32[33,128,128]{2,1,0:T(8,128)S(1)} %get-tuple-element.98.refs_0_, f32[33,128,128]{2,1,0:T(8,128)S(1)} %get-tuple-element.103.refs_1_), custom_call_target="tpu_custom_call" | custom-call | tf_op jit(solution)/shard_map/cond/branch_1_fun/users/pallas_call | solution.py:256
  125.6 5.1 %collective-permute-done.45.refs_3_ = f32[512,128]{1,0:T(8,128)S(1)} collective-permute-done((f32[512,128]{1,0:T(8,128)S(1)}, f32[512,128]{1,0:T(8,128)S(1)}, u32[]{:S(2)}, u32[]{:S(2)}) %collective-permute-start.45) | collective-permute-done | bytes 262176 | tf_op jit(solution)/shard_map/cond/branch_1_fun/ppermute | solution.py:325
  (52 shorter events, 21.5 us)
Async XLA Ops:
  11.4 8.6 %collective-permute-start.27 = (f32[520,128]{1,0:T(8,128)S(1)}, f32[520,128]{1,0:T(8,128)S(1)}, u32[]{:S(2)}, u32[]{:S(2)}) collective-permute-start(f32[520,128]{1,0:T(8,128)S(1)} %get-tuple-element.97), channel_id=1, source_target_pairs={{0,1},{1,0},{2,3},{3,2},{4,5},{5,4},{6,7},{7,6},{8,9},{9,8},{10,11... | collective-permute-start | bytes 798728 | tf_op jit(solution)/shard_map/cond/branch_1_fun/ppermute | solution.py:325
  19.5 7.7 %collective-permute-start.26 = (f32[520,128]{1,0:T(8,128)S(1)}, f32[520,128]{1,0:T(8,128)S(1)}, u32[]{:S(2)}, u32[]{:S(2)}) collective-permute-start(f32[520,128]{1,0:T(8,128)S(1)} %get-tuple-element.95), channel_id=1, source_target_pairs={{0,1},{1,0},{2,3},{3,2},{4,5},{5,4},{6,7},{7,6},{8,9},{9,8},{10,11... | collective-permute-start | bytes 798728 | tf_op jit(solution)/shard_map/cond/branch_1_fun/ppermute | solution.py:325
  20.1 12.7 %collective-permute-start.28 = (f32[520,128]{1,0:T(8,128)S(1)}, f32[520,128]{1,0:T(8,128)S(1)}, u32[]{:S(2)}, u32[]{:S(2)}) collective-permute-start(f32[520,128]{1,0:T(8,128)S(1)} %add.38), channel_id=1, source_target_pairs={{0,2},{1,3},{2,0},{3,1},{4,6},{5,7},{6,4},{7,5},{8,10},{9,11},{10,... | collective-permute-start | bytes 798728 | tf_op jit(solution)/shard_map/cond/branch_1_fun/ppermute | solution.py:325
  22.0 16.5 %collective-permute-start.33 = (f32[520,128]{1,0:T(8,128)S(1)}, f32[520,128]{1,0:T(8,128)S(1)}, u32[]{:S(2)}, u32[]{:S(2)}) collective-permute-start(f32[520,128]{1,0:T(8,128)S(1)} %get-tuple-element.100), channel_id=1, source_target_pairs={{0,2},{1,3},{2,0},{3,1},{4,6},{5,7},{6,4},{7,5},{8,10},{9,11},{10,... | collective-permute-start | bytes 798728 | tf_op jit(solution)/shard_map/cond/branch_1_fun/ppermute | solution.py:325
  27.1 11.4 %collective-permute-start.35 = (f32[520,128]{1,0:T(8,128)S(1)}, f32[520,128]{1,0:T(8,128)S(1)}, u32[]{:S(2)}, u32[]{:S(2)}) collective-permute-start(f32[520,128]{1,0:T(8,128)S(1)} %add.39), channel_id=1, source_target_pairs={{0,1},{1,0},{2,3},{3,2},{4,5},{5,4},{6,7},{7,6},{8,9},{9,8},{10,11... | collective-permute-start | bytes 798728 | tf_op jit(solution)/shard_map/cond/branch_1_fun/ppermute | solution.py:325
  38.5 17.0 %collective-permute-start.36 = (f32[512,128]{1,0:T(8,128)S(1)}, f32[512,128]{1,0:T(8,128)S(1)}, u32[]{:S(2)}, u32[]{:S(2)}) collective-permute-start(f32[512,128]{1,0:T(8,128)S(1)} %items.21), channel_id=1, source_target_pairs={{0,20},{4,16},{8,28},{12,24},{16,4},{20,0},{24,12},{28,8},{1,21},{... | collective-permute-start | bytes 786440 | tf_op jit(solution)/shard_map/cond/branch_1_fun/ppermute | solution.py:325
  39.7 17.9 %collective-permute-start.31 = (f32[512,128]{1,0:T(8,128)S(1)}, f32[512,128]{1,0:T(8,128)S(1)}, u32[]{:S(2)}, u32[]{:S(2)}) collective-permute-start(f32[512,128]{1,0:T(8,128)S(1)} %collective-permute-done.29.refs_0_.old_ref), channel_id=1, source_target_pairs={{0,2},{1,3},{2,0},{3,1},{4,6},{5,7},{6,4},{7,5},{8,10},{9,11},{10,... | collective-permute-start | bytes 786440 | tf_op jit(solution)/shard_map/cond/branch_1_fun/ppermute | solution.py:325
  55.6 8.4 %collective-permute-start.37 = (f32[512,128]{1,0:T(8,128)S(1)}, f32[512,128]{1,0:T(8,128)S(1)}, u32[]{:S(2)}, u32[]{:S(2)}) collective-permute-start(f32[512,128]{1,0:T(8,128)S(1)} %collective-permute-done.36.refs_0_.old_ref), channel_id=1, source_target_pairs={{0,1},{1,0},{2,3},{3,2},{4,5},{5,4},{6,7},{7,6},{8,9},{9,8},{10,11... | collective-permute-start | bytes 786440 | tf_op jit(solution)/shard_map/cond/branch_1_fun/ppermute | solution.py:325
  55.6 14.0 %collective-permute-start.30 = (f32[512,128]{1,0:T(8,128)S(1)}, f32[512,128]{1,0:T(8,128)S(1)}, u32[]{:S(2)}, u32[]{:S(2)}) collective-permute-start(f32[512,128]{1,0:T(8,128)S(1)} %collective-permute-done.29.refs_0_.old_ref), channel_id=1, source_target_pairs={{0,1},{1,0},{2,3},{3,2},{4,5},{5,4},{6,7},{7,6},{8,9},{9,8},{10,11... | collective-permute-start | bytes 786440 | tf_op jit(solution)/shard_map/cond/branch_1_fun/ppermute | solution.py:325
  57.6 17.6 %collective-permute-start.32 = (f32[512,128]{1,0:T(8,128)S(1)}, f32[512,128]{1,0:T(8,128)S(1)}, u32[]{:S(2)}, u32[]{:S(2)}) collective-permute-start(f32[512,128]{1,0:T(8,128)S(1)} %collective-permute-done.31.refs_2_), channel_id=1, source_target_pairs={{0,1},{1,0},{2,3},{3,2},{4,5},{5,4},{6,7},{7,6},{8,9},{9,8},{10,11... | collective-permute-start | bytes 786440 | tf_op jit(solution)/shard_map/cond/branch_1_fun/ppermute | solution.py:325
  59.4 23.9 %collective-permute-start.38 = (f32[512,128]{1,0:T(8,128)S(1)}, f32[512,128]{1,0:T(8,128)S(1)}, u32[]{:S(2)}, u32[]{:S(2)}) collective-permute-start(f32[512,128]{1,0:T(8,128)S(1)} %collective-permute-done.36.refs_0_.old_ref), channel_id=1, source_target_pairs={{0,2},{1,3},{2,0},{3,1},{4,6},{5,7},{6,4},{7,5},{8,10},{9,11},{10,... | collective-permute-start | bytes 786440 | tf_op jit(solution)/shard_map/cond/branch_1_fun/ppermute | solution.py:325
  64.0 19.3 %collective-permute-start.39 = (f32[512,128]{1,0:T(8,128)S(1)}, f32[512,128]{1,0:T(8,128)S(1)}, u32[]{:S(2)}, u32[]{:S(2)}) collective-permute-start(f32[512,128]{1,0:T(8,128)S(1)} %collective-permute-done.37.refs_1_), channel_id=1, source_target_pairs={{0,2},{1,3},{2,0},{3,1},{4,6},{5,7},{6,4},{7,5},{8,10},{9,11},{10,... | collective-permute-start | bytes 786440 | tf_op jit(solution)/shard_map/cond/branch_1_fun/ppermute | solution.py:325
  81.4 12.0 %collective-permute-start.41 = (f32[520,128]{1,0:T(8,128)S(1)}, f32[520,128]{1,0:T(8,128)S(1)}, u32[]{:S(2)}, u32[]{:S(2)}) collective-permute-start(f32[520,128]{1,0:T(8,128)S(1)} %get-tuple-element.107), channel_id=1, source_target_pairs={{0,1},{1,0},{2,3},{3,2},{4,5},{5,4},{6,7},{7,6},{8,9},{9,8},{10,11... | collective-permute-start | bytes 798728 | tf_op jit(solution)/shard_map/cond/branch_1_fun/ppermute | solution.py:325
  89.5 8.5 %collective-permute-start.47 = (f32[520,128]{1,0:T(8,128)S(1)}, f32[520,128]{1,0:T(8,128)S(1)}, u32[]{:S(2)}, u32[]{:S(2)}) collective-permute-start(f32[520,128]{1,0:T(8,128)S(1)} %get-tuple-element.111), channel_id=1, source_target_pairs={{0,2},{1,3},{2,0},{3,1},{4,6},{5,7},{6,4},{7,5},{8,10},{9,11},{10,... | collective-permute-start | bytes 798728 | tf_op jit(solution)/shard_map/cond/branch_1_fun/ppermute | solution.py:325
  89.8 11.6 %collective-permute-start.40 = (f32[520,128]{1,0:T(8,128)S(1)}, f32[520,128]{1,0:T(8,128)S(1)}, u32[]{:S(2)}, u32[]{:S(2)}) collective-permute-start(f32[520,128]{1,0:T(8,128)S(1)} %get-tuple-element.105), channel_id=1, source_target_pairs={{0,1},{1,0},{2,3},{3,2},{4,5},{5,4},{6,7},{7,6},{8,9},{9,8},{10,11... | collective-permute-start | bytes 798728 | tf_op jit(solution)/shard_map/cond/branch_1_fun/ppermute | solution.py:325
  93.5 10.3 %collective-permute-start.42 = (f32[520,128]{1,0:T(8,128)S(1)}, f32[520,128]{1,0:T(8,128)S(1)}, u32[]{:S(2)}, u32[]{:S(2)}) collective-permute-start(f32[520,128]{1,0:T(8,128)S(1)} %add.40), channel_id=1, source_target_pairs={{0,2},{1,3},{2,0},{3,1},{4,6},{5,7},{6,4},{7,5},{8,10},{9,11},{10,... | collective-permute-start | bytes 798728 | tf_op jit(solution)/shard_map/cond/branch_1_fun/ppermute | solution.py:325
  94.1 15.3 %collective-permute-start.46 = (f32[520,128]{1,0:T(8,128)S(1)}, f32[520,128]{1,0:T(8,128)S(1)}, u32[]{:S(2)}, u32[]{:S(2)}) collective-permute-start(f32[520,128]{1,0:T(8,128)S(1)} %get-tuple-element.109), channel_id=1, source_target_pairs={{0,2},{1,3},{2,0},{3,1},{4,6},{5,7},{6,4},{7,5},{8,10},{9,11},{10,... | collective-permute-start | bytes 798728 | tf_op jit(solution)/shard_map/cond/branch_1_fun/ppermute | solution.py:325
  98.0 11.4 %collective-permute-start.48 = (f32[520,128]{1,0:T(8,128)S(1)}, f32[520,128]{1,0:T(8,128)S(1)}, u32[]{:S(2)}, u32[]{:S(2)}) collective-permute-start(f32[520,128]{1,0:T(8,128)S(1)} %add.41), channel_id=1, source_target_pairs={{0,1},{1,0},{2,3},{3,2},{4,5},{5,4},{6,7},{7,6},{8,9},{9,8},{10,11... | collective-permute-start | bytes 798728 | tf_op jit(solution)/shard_map/cond/branch_1_fun/ppermute | solution.py:325
  103.8 11.2 %collective-permute-start.44 = (f32[512,128]{1,0:T(8,128)S(1)}, f32[512,128]{1,0:T(8,128)S(1)}, u32[]{:S(2)}, u32[]{:S(2)}) collective-permute-start(f32[512,128]{1,0:T(8,128)S(1)} %items.22.refs_0_), channel_id=1, source_target_pairs={{0,2},{1,3},{2,0},{3,1},{4,6},{5,7},{6,4},{7,5},{8,10},{9,11},{10,... | collective-permute-start | bytes 786440 | tf_op jit(solution)/shard_map/cond/branch_1_fun/ppermute | solution.py:325
  109.5 10.5 %collective-permute-start.49 = (f32[512,128]{1,0:T(8,128)S(1)}, f32[512,128]{1,0:T(8,128)S(1)}, u32[]{:S(2)}, u32[]{:S(2)}) collective-permute-start(f32[512,128]{1,0:T(8,128)S(1)} %items.23.refs_4_), channel_id=1, source_target_pairs={{0,1},{1,0},{2,3},{3,2},{4,5},{5,4},{6,7},{7,6},{8,9},{9,8},{10,11... | collective-permute-start | bytes 786440 | tf_op jit(solution)/shard_map/cond/branch_1_fun/ppermute | solution.py:325
  112.9 12.7 %collective-permute-start.43 = (f32[512,128]{1,0:T(8,128)S(1)}, f32[512,128]{1,0:T(8,128)S(1)}, u32[]{:S(2)}, u32[]{:S(2)}) collective-permute-start(f32[512,128]{1,0:T(8,128)S(1)} %items.22.refs_0_), channel_id=1, source_target_pairs={{0,1},{1,0},{2,3},{3,2},{4,5},{5,4},{6,7},{7,6},{8,9},{9,8},{10,11... | collective-permute-start | bytes 786440 | tf_op jit(solution)/shard_map/cond/branch_1_fun/ppermute | solution.py:325
  113.0 12.6 %collective-permute-start.50 = (f32[512,128]{1,0:T(8,128)S(1)}, f32[512,128]{1,0:T(8,128)S(1)}, u32[]{:S(2)}, u32[]{:S(2)}) collective-permute-start(f32[512,128]{1,0:T(8,128)S(1)} %items.23.refs_4_), channel_id=1, source_target_pairs={{0,2},{1,3},{2,0},{3,1},{4,6},{5,7},{6,4},{7,5},{8,10},{9,11},{10,... | collective-permute-start | bytes 786440 | tf_op jit(solution)/shard_map/cond/branch_1_fun/ppermute | solution.py:325
  115.0 15.7 %collective-permute-start.45 = (f32[512,128]{1,0:T(8,128)S(1)}, f32[512,128]{1,0:T(8,128)S(1)}, u32[]{:S(2)}, u32[]{:S(2)}) collective-permute-start(f32[512,128]{1,0:T(8,128)S(1)} %collective-permute-done.44.refs_2_), channel_id=1, source_target_pairs={{0,1},{1,0},{2,3},{3,2},{4,5},{5,4},{6,7},{7,6},{8,9},{9,8},{10,11... | collective-permute-start | bytes 786440 | tf_op jit(solution)/shard_map/cond/branch_1_fun/ppermute | solution.py:325
  120.0 10.7 %collective-permute-start.51 = (f32[512,128]{1,0:T(8,128)S(1)}, f32[512,128]{1,0:T(8,128)S(1)}, u32[]{:S(2)}, u32[]{:S(2)}) collective-permute-start(f32[512,128]{1,0:T(8,128)S(1)} %collective-permute-done.49.refs_5_), channel_id=1, source_target_pairs={{0,2},{1,3},{2,0},{3,1},{4,6},{5,7},{6,4},{7,5},{8,10},{9,11},{10,... | collective-permute-start | bytes 786440 | tf_op jit(solution)/shard_map/cond/branch_1_fun/ppermute | solution.py:325
  (5 other events, 61.7 us)
where the time goes:
time: 135 us; the launch traced here: 133 us
  waiting for transfers between devices  67.6 us (50%)
  Pallas kernels  33.7 us (25%)
  starting transfers between devices  28.2 us (21%)
  between operations  1.5 us (1%)
    ppermute x26, waiting for transfers between devices, swap(): lax.ppermute(value, axis, [(i, i ^ mask) for i in range(lax.axis_size(axi...  67.6 us
    ppermute x26, starting transfers between devices, swap(): lax.ppermute(value, axis, [(i, i ^ mask) for i in range(lax.axis_size(axi...  28.2 us
    pallas_call x4, Pallas kernels, slot_terms(): pl.pallas_call(functools.partial(slots_kernel, lay, epoch, chunk, len(blo...  24.7 us
    pallas_call x2, Pallas kernels, user_step(): pl.pallas_call(functools.partial(user_kernel, lay, epoch, last), out_shap...  4.18 us
    pallas_call x1, Pallas kernels, prepare(): pl.pallas_call(functools.partial(prepare_kernel, lay, epochs), out_shape=...  3.07 us
  transfers between devices with their start and end apart: 26, of which 16 were waited for; matrix products, arithmetic and copies ran while one was open for 0% of the time, Pallas kernels for 17%

commit v1 on v0

v1 whole, which is shorter than its diff:
```python
import functools

import jax
import jax.numpy as jnp
from jax import lax
from jax.experimental import pallas as pl
from jax.experimental.pallas import tpu as pltpu
from jax.sharding import PartitionSpec as P

LEARNING_RATE = 0.05
WEIGHT_DECAY = 0.05
KEEP = 1.0 - LEARNING_RATE * WEIGHT_DECAY

TILE = 128
SPLIT = (1, 1)
LANES = (1, 2)
DIRECT_SUM = ((1, 1), (0, 0))
DIRECT_SPREAD = ((1, 1), (0, 0))
UNITS = 8
STEP = 2 * UNITS
AHEAD = 3
RING = 4
FIELD = 6
COUNT_ROWS = 8
VMEM_BYTES = 24 << 20
SLOT_VMEM_BYTES = 44 << 20

CONTRACT_LAST = (((1,), (1,)), ((), ()))
VMEM = pl.BlockSpec(memory_space=pltpu.VMEM)
SMEM = pl.BlockSpec(memory_space=pltpu.SMEM)
ANY = pl.BlockSpec(memory_space=pl.ANY)
PARAMS = pltpu.CompilerParams(vmem_limit_bytes=VMEM_BYTES)


def up(value, unit):
    return (value + unit - 1) // unit * unit


class Lane:
    def __init__(self, chunk_first, share, lane, lanes, replicas):
        self.chunk_first, self.share, self.replicas = chunk_first, share, replicas
        self.tiles = share // lanes
        self.skip = lane * self.tiles
        self.rows = self.tiles * TILE
        self.sent = self.rows + COUNT_ROWS
        levels = replicas.bit_length() - 1
        self.bits = [1 << (lane + i) % levels for i in range(levels)]

    def arrays(self, direct):
        if direct:
            return [[k] for k in range(self.replicas)]
        order = sorted(range(self.replicas), key=lambda k: [k & bit for bit in self.bits])
        return [order[: self.replicas // 2], order[self.replicas // 2 :]]

    def first(self, me, k):
        return lax.bitwise_xor(me, k) * self.share + self.skip


class Layout:
    def __init__(self, users, items, slots, replicas):
        self.users, self.items, self.slots, self.replicas = users, items, slots, replicas
        self.tiles = [items * part // sum(SPLIT) for part in SPLIT]
        self.firsts = [sum(self.tiles[:c]) for c in range(len(SPLIT))]
        self.chunks = len(SPLIT)
        self.lanes = []
        for wanted in LANES:
            self.lanes.append([])
            for c in range(self.chunks):
                share = self.tiles[c] // replicas
                lanes = wanted if share % wanted == 0 else 1
                self.lanes[-1].append([Lane(self.firsts[c], share, n, lanes, replicas) for n in range(lanes)])
        self.groups = self.chunks * users
        self.group_cols = up(self.groups + 1, 128)
        self.steps = up((slots + self.groups) // STEP + self.chunks + AHEAD + 1, 8)
        self.start_at = self.steps
        self.count_at = self.start_at + self.group_cols // 128
        self.seen_at = self.count_at + 1
        self.table_rows = up(self.seen_at + 1, 8)

    def start(self, table_ref, epoch, chunk):
        at = chunk * self.users
        row = lax.shift_right_logical(at, 7)
        return table_ref[epoch * self.table_rows + self.start_at + row, lax.bitwise_and(at, 127)]


def column(row, across):
    return jnp.broadcast_to(row, (across, row.shape[1])).T


def low_tiles(rows, low_ref, lowt_ref, a):
    low_ref[a] = rows.astype(jnp.bfloat16)
    lowt_ref[a] = rows.T.astype(jnp.bfloat16)


def slot_table(lay, user, item, live):
    def iota(shape, axis):
        return lax.broadcasted_iota(jnp.int32, shape, axis)

    def total(mask, values=1):
        return jnp.sum(jnp.where(mask, values, 0), axis=0, keepdims=True)

    n, groups, users = lay.slots, lay.group_cols, lay.users
    chunk = sum((item >= first).astype(jnp.int32) for first in lay.firsts[1:]) + jnp.zeros_like(item)
    local = item - sum(jnp.where(chunk == c, first, 0) for c, first in enumerate(lay.firsts))
    group = jnp.where(live, chunk * users + user, lay.groups)
    packed = user + (local << FIELD) + (iota((1, n), 1) << 2 * FIELD)
    same = column(group, n) == group
    rank = total(same & (iota((n, n), 0) < iota((n, n), 1)))
    count = total(column(group, groups) == iota((n, groups), 1))
    padded = column((count + 1) // 2 * 2, groups)
    above, here = iota((groups, groups), 0), iota((groups, groups), 1)
    inside = total((above < here) & (above // users == here // users), padded)
    steps = (total(above // users == here // users, padded) + STEP - 1) // STEP
    start = total((above % users == 0) & (above // users < here // users), column(steps, groups))
    base = start * STEP + inside
    place = rank + total(iota((groups, n), 0) == group, column(base, n))
    place = jnp.where(live, place, -1)
    every = iota((1, groups), 1)
    spare = jnp.where((count % 2 == 1) & (every < lay.groups), base + count, -1)
    pad = sum(jnp.where(every // users == c, tiles, 0) for c, tiles in enumerate(lay.tiles))
    cols = lay.steps * STEP
    cols = up(cols, 128)
    order = total(column(place, cols) == iota((n, cols), 1), column(packed - users, cols))
    order += total(column(spare, cols) == iota((groups, cols), 1), column(every % users - users + (pad << FIELD), cols))
    order += users
    seen_user = total(column(jnp.where(live, user, -1), 128) == iota((n, 128), 1))
    seen_item = total(column(jnp.where(live, item, -1), 128) == iota((n, 128), 1))
    return order, start, seen_user, seen_item


def prepare_kernel(lay, epochs, user_ref, item_ref, live_ref, rows_hbm, table_ref, low_ref, lowt_ref, rows_ref, sems):
    parts = sems.shape[0]
    height = rows_ref.shape[0] // parts
    copies = []
    for p in range(parts):
        at = pl.ds(p * height, height)
        copies.append(pltpu.make_async_copy(rows_hbm.at[at, :], rows_ref.at[at, :], sems.at[p]))
        copies[-1].start()
    for e in range(epochs):
        live = lax.broadcasted_iota(jnp.int32, (1, lay.slots), 1) < live_ref[:, e : e + 1]
        order, start, seen_user, seen_item = slot_table(lay, user_ref[e : e + 1, :], item_ref[e : e + 1, :], live)
        top = e * lay.table_rows
        mask = (1 << FIELD) - 1
        for at, values in ((0, order >> 2 * FIELD), (STEP, order & mask), (2 * STEP, (order >> FIELD) & mask)):
            for g in range(lay.steps):
                table_ref[top + g : top + g + 1, at : at + STEP] = values[:, g * STEP : (g + 1) * STEP]
        for n in range(lay.group_cols // 128):
            table_ref[top + lay.start_at + n : top + lay.start_at + n + 1, :] = start[:, n * 128 : (n + 1) * 128]
        table_ref[top + lay.count_at : top + lay.count_at + 1, :] = seen_user
        table_ref[top + lay.seen_at : top + lay.seen_at + 1, :] = seen_item
    low_ref[lay.users] = jnp.zeros((TILE, TILE), jnp.bfloat16)
    lowt_ref[lay.users] = jnp.zeros((TILE, TILE), jnp.bfloat16)
    share = lay.users // parts
    for p in range(parts):
        copies[p].wait()

        def lower(i, _, p=p):
            a = p * share + i
            low_tiles(rows_ref[pl.ds(pl.multiple_of(a * TILE, TILE), TILE), :], low_ref, lowt_ref, a)
            return 0

        lax.fori_loop(0, share, lower, 0, unroll=4)


def low_shape(lay):
    return jax.ShapeDtypeStruct((lay.users + 1, TILE, TILE), jnp.bfloat16)


def prepare(lay, user_tile, item_tile, live_count, user_rows):
    epochs = user_tile.shape[0]
    parts = 4
    return pl.pallas_call(
        functools.partial(prepare_kernel, lay, epochs),
        out_shape=[
            jax.ShapeDtypeStruct((epochs * lay.table_rows, 128), jnp.int32),
            low_shape(lay),
            low_shape(lay),
        ],
        in_specs=[VMEM, VMEM, VMEM, ANY],
        out_specs=[VMEM] * 3,
        scratch_shapes=[pltpu.VMEM(user_rows.shape, jnp.float32), pltpu.SemaphoreType.DMA((parts,))],
        compiler_params=PARAMS,
        name="prepare",
    )(user_tile, item_tile, live_count, user_rows)


def slots_kernel(
    lay, sources, targets, tiles, table_ref, me_ref, where_ref, ratings_ref, low_ref, lowt_ref, *refs
):
    count_in = sum(len(arrays) for _, arrays in sources) if sources else 1
    count_out = sum(len(arrays) for _, arrays in targets)
    block_refs, refs = refs[:count_in], refs[count_in:]
    user_grad, piece_refs = refs[0], refs[1 : 1 + count_out]
    buf, sems, item_low, item_grad = refs[1 + count_out :]
    me, epoch, chunk, chunk_first = me_ref[0], where_ref[0], where_ref[1], where_ref[2]
    top = epoch * lay.table_rows + lay.start(table_ref, epoch, chunk)
    steps = lay.start(table_ref, epoch, chunk + 1) - lay.start(table_ref, epoch, chunk)
    zero = jnp.zeros((TILE, TILE), jnp.float32)

    def fetch(g):
        ring = lax.bitwise_and(g, RING - 1)
        for s in range(STEP):
            slot = table_ref[top + g, s]
            pltpu.make_async_copy(ratings_ref.at[epoch, slot], buf.at[ring, s], sems.at[ring]).start()

    def land(g):
        ring = lax.bitwise_and(g, RING - 1)
        pltpu.make_async_copy(ratings_ref.at[epoch, pl.ds(0, STEP)], buf.at[ring], sems.at[ring]).wait()

    def fetch_first(g, _):
        fetch(g)
        return 0

    lax.fori_loop(0, AHEAD, fetch_first, 0)

    if sources:
        inputs = iter(block_refs)
        for lane, arrays in sources:
            for pieces in arrays:
                block = next(inputs)
                for n, k in enumerate(pieces):
                    first = lane.first(me, k)
                    for j in range(lane.tiles):
                        at = n * lane.rows + j * TILE
                        item_low[first + j] = block[at : at + TILE, :].astype(jnp.bfloat16)
    else:


        def lower(j, _):
            at = pl.ds(pl.multiple_of((chunk_first + j) * TILE, TILE), TILE)
            item_low[j] = block_refs[0][at, :].astype(jnp.bfloat16)
            return 0

        lax.fori_loop(0, tiles, lower, 0, unroll=4)
    item_low[tiles] = jnp.zeros((TILE, TILE), jnp.bfloat16)

    def clear_item(a, _):
        item_grad[a] = zero
        return 0

    def clear_user(a, _):
        user_grad[a] = zero
        return 0

    lax.fori_loop(0, tiles, clear_item, 0, unroll=4)
    lax.fori_loop(0, lay.users, clear_user, 0, unroll=4)

    def step(g, _):
        land(g)
        fetch(g + AHEAD)
        ring = lax.bitwise_and(g, RING - 1)
        units = []
        for n in range(UNITS):
            user = table_ref[top + g, STEP + 2 * n]
            items = [table_ref[top + g, 2 * STEP + 2 * n + s] for s in range(2)]
            right = jnp.concatenate([item_low[b] for b in items], axis=0)
            predicted = lax.dot_general(low_ref[user], right, CONTRACT_LAST, preferred_element_type=jnp.float32)
            rating = jnp.concatenate([buf[ring, 2 * n + s] for s in range(2)], axis=1)
            residual = (rating.astype(jnp.float32) - predicted).astype(jnp.bfloat16)
            units.append((user, items, right, residual))
        for user, items, right, residual in units:
            user_grad[user] += jnp.dot(residual, right, preferred_element_type=jnp.float32)
            part = jnp.dot(lowt_ref[user], residual, preferred_element_type=jnp.float32)
            for s in range(2):
                item_grad[items[s]] += part[:, s * TILE : (s + 1) * TILE]
        return 0

    lax.fori_loop(0, steps, step, 0)

    def turn(j, _):
        item_grad[j] = item_grad[j].T
        return 0

    lax.fori_loop(0, tiles, turn, 0, unroll=2)
    row = lax.broadcasted_iota(jnp.int32, (COUNT_ROWS, TILE), 0)
    outputs = iter(piece_refs)
    for lane, arrays in targets:
        for pieces in arrays:
            out = next(outputs)
            for n, k in enumerate(pieces):
                first = lane.first(me, k)
                counts = jnp.zeros((COUNT_ROWS, TILE), jnp.int32)
                for j in range(lane.tiles):
                    at = n * lane.sent + j * TILE
                    out[at : at + TILE, :] = item_grad[first + j]
                    seen = table_ref[epoch * lay.table_rows + lay.seen_at, chunk_first + first + j]
                    counts = jnp.where(row == j, seen, counts)
                at = n * lane.sent + lane.rows
                out[at : at + COUNT_ROWS, :] = counts.astype(jnp.float32)

    def drain(g, _):
        land(steps + g)
        return 0

    lax.fori_loop(0, AHEAD, drain, 0)


def routes(lay, direct, epoch, chunk):
    return [(lane, lane.arrays(direct[epoch][chunk])) for lane in lay.lanes[epoch][chunk]]


def slot_terms(lay, epoch, chunk, table, me, ratings, low, lowt, blocks):
    sources = routes(lay, DIRECT_SPREAD, epoch - 1, chunk) if epoch else None
    targets = routes(lay, DIRECT_SUM, epoch, chunk)
    pieces = [
        jax.ShapeDtypeStruct((len(held) * lane.sent, TILE), jnp.float32)
        for lane, arrays in targets
        for held in arrays
    ]
    user_grad = jax.ShapeDtypeStruct((lay.users + 1, TILE, TILE), jnp.float32)
    live = lay.slots // lay.chunks
    where = jnp.array([epoch, chunk, lay.firsts[chunk]], jnp.int32)
    out = pl.pallas_call(
        functools.partial(slots_kernel, lay, sources, targets, lay.tiles[chunk]),
        out_shape=[user_grad] + pieces,
        in_specs=[SMEM, SMEM, SMEM, ANY, VMEM, VMEM] + [VMEM] * len(blocks),
        out_specs=[VMEM] * (1 + len(pieces)),
        scratch_shapes=[
            pltpu.VMEM((RING, STEP, TILE, TILE), jnp.bfloat16),
            pltpu.SemaphoreType.DMA((RING,)),
            pltpu.VMEM((lay.tiles[chunk] + 1, TILE, TILE), jnp.bfloat16),
            pltpu.VMEM((lay.tiles[chunk] + 1, TILE, TILE), jnp.float32),
        ],
        cost_estimate=pl.CostEstimate(
            flops=6 * live * TILE**3 * 4, bytes_accessed=live * TILE * TILE * 2, transcendentals=0
        ),
        compiler_params=pltpu.CompilerParams(vmem_limit_bytes=SLOT_VMEM_BYTES),
        name="slots",
    )(table, me, where, ratings, low, lowt, *blocks)
    parts = iter(out[1:])
    return out[0], [[next(parts) for _ in arrays] for _, arrays in targets]


def user_kernel(lay, epoch, last, table_ref, rows_ref, *refs):
    grads, refs = refs[: lay.chunks], refs[lay.chunks :]

    def one(a, _):
        seen = table_ref[epoch * lay.table_rows + lay.count_at, a]
        seen = jnp.maximum(jnp.broadcast_to(seen, (1, TILE)).astype(jnp.float32), 1.0)
        at = pl.ds(pl.multiple_of(a * TILE, TILE), TILE)
        grad = sum(grad_ref[a] for grad_ref in grads)
        rows = rows_ref[at, :] * KEEP + grad * (LEARNING_RATE / seen)
        refs[0][at, :] = rows
        if not last:
            low_tiles(rows, refs[1], refs[2], a)
        return 0

    lax.fori_loop(0, lay.users, one, 0, unroll=4)
    if not last:
        refs[1][lay.users] = jnp.zeros((TILE, TILE), jnp.bfloat16)
        refs[2][lay.users] = jnp.zeros((TILE, TILE), jnp.bfloat16)


def user_step(lay, epoch, last, table, rows, grads):
    out_shape = [jax.ShapeDtypeStruct(rows.shape, jnp.float32)]
    if not last:
        out_shape += [low_shape(lay)] * 2
    return pl.pallas_call(
        functools.partial(user_kernel, lay, epoch, last),
        out_shape=out_shape,
        in_specs=[SMEM] + [VMEM] * (1 + len(grads)),
        out_specs=[VMEM] * len(out_shape),
        compiler_params=PARAMS,
        name="users",
    )(table, rows, *grads)


def item_kernel(lane, whole, skip, me_ref, old_ref, *refs):
    parts, out_ref = refs[:-1], refs[-1]
    first = lane.chunk_first + lane.first(me_ref[0], 0) if whole else skip
    for j in range(lane.tiles):
        at = slice(j * TILE, (j + 1) * TILE)
        from_tile = (first + j) * TILE
        old = old_ref[pl.ds(pl.multiple_of(from_tile, TILE) if whole else from_tile, TILE), :]
        row = lane.rows + j
        seen = jnp.maximum(sum(part[row : row + 1, :] for part in parts), 1.0)
        grad = sum(part[at, :] for part in parts)
        out_ref[at, :] = old * KEEP + grad * (LEARNING_RATE / seen)


def item_step(lane, whole, skip, me, old, parts):
    return pl.pallas_call(
        functools.partial(item_kernel, lane, whole, skip),
        out_shape=jax.ShapeDtypeStruct((lane.rows, TILE), jnp.float32),
        in_specs=[SMEM] + [VMEM] * (1 + len(parts)),
        out_specs=VMEM,
        compiler_params=PARAMS,
        name="items",
    )(me, old, *parts)


def assemble_kernel(lay, sources, me_ref, *refs):
    arrays, out_ref, sems = iter(refs[:-2]), refs[-2], refs[-1]
    copies = []
    for held in sources:
        for lane, groups in held:
            for pieces in groups:
                array = next(arrays)
                for n, k in enumerate(pieces):
                    first = (lane.chunk_first + lane.first(me_ref[0], k)) * TILE
                    at = pl.ds(pl.multiple_of(first, TILE), lane.rows)
                    sem = sems.at[len(copies)]
                    piece = array.at[pl.ds(n * lane.rows, lane.rows), :]
                    copies.append(pltpu.make_async_copy(piece, out_ref.at[at, :], sem))
                    copies[-1].start()
    for copy in copies:
        copy.wait()


def assemble(lay, epoch, me, arrays):
    sources = [routes(lay, DIRECT_SPREAD, epoch, c) for c in range(lay.chunks)]
    count = sum(len(pieces) for held in sources for _, groups in held for pieces in groups)
    return pl.pallas_call(
        functools.partial(assemble_kernel, lay, sources),
        out_shape=jax.ShapeDtypeStruct((lay.items * TILE, TILE), jnp.float32),
        in_specs=[SMEM] + [VMEM] * len(arrays),
        out_specs=ANY,
        scratch_shapes=[pltpu.SemaphoreType.DMA((count,))],
        compiler_params=PARAMS,
        name="assemble",
    )(me, *arrays)


def swap(value, axis, mask):
    return lax.ppermute(value, axis, [(i, i ^ mask) for i in range(lax.axis_size(axis))])


def gather_sum(lane, direct, arrays):
    if direct:
        return [arrays[0]] + [swap(array, "replica", k) for k, array in enumerate(arrays) if k]
    parts, leave, held = [arrays[0]], arrays[1], lane.replicas
    for bit in lane.bits:
        held //= 2
        if held < lane.replicas // 2:
            half = slice(held * lane.sent, 2 * held * lane.sent)
            leave = functools.reduce(jnp.add, [part[half] for part in parts])
        parts.append(swap(leave, "replica", bit))
    return parts


def spread(lane, direct, own):
    if direct:
        return [own] + [swap(own, "replica", k) for k in range(1, lane.replicas)]
    held = own
    for bit in reversed(lane.bits[1:]):
        held = jnp.concatenate([held, swap(held, "replica", bit)], axis=0)
    return [held, swap(held, "replica", lane.bits[0])]


def steps(flip, lay, user_factors, item_factors, ratings, user_tile, item_tile, live_count):
    me = lax.axis_index("replica").astype(jnp.int32).reshape(1)
    epochs = ratings.shape[0]
    rows = user_factors
    table, low, lowt = prepare(lay, user_tile, item_tile, live_count.T, rows)
    blocks = [[[item_factors]]] * lay.chunks
    for e in range(epochs):
        last = e + 1 == epochs
        grads, parts = [], []
        for c in range(lay.chunks):
            block = [array for arrays in blocks[c] for array in arrays]
            grad, pieces = slot_terms(lay, e, c, table, me, ratings, low, lowt, block)
            grads.append(grad)
            parts.append([gather_sum(lane, DIRECT_SUM[e][c], held) for lane, held in zip(lay.lanes[e][c], pieces)])
        if last:
            (rows,) = user_step(lay, e, last, table, rows, grads)
        else:
            rows, low, lowt = user_step(lay, e, last, table, rows, grads)
        fresh = []
        for c in range(lay.chunks):
            lanes = []
            for n, lane in enumerate(lay.lanes[e][c]):
                same = len(blocks[c]) == len(lay.lanes[e][c])
                old = blocks[c][n if same else 0][0]
                own = item_step(lane, e == 0, 0 if same else lane.skip, me, old, parts[c][n])
                if not last:
                    own = swap(own, "stratum", flip)
                lanes.append(spread(lane, DIRECT_SPREAD[e][c], own))
            fresh.append(lanes)
        blocks = fresh
    arrays = [array for lanes in blocks for held in lanes for array in held]
    return rows, assemble(lay, epochs - 1, me, arrays)


def local(user_factors, item_factors, ratings, user_tile, item_tile, live_count, partner):
    users, items = user_factors.shape[0] // TILE, item_factors.shape[0] // TILE
    replicas, strata = lax.axis_size("replica"), lax.axis_size("stratum")
    lay = Layout(users, items, ratings.shape[1], replicas)
    branches = [functools.partial(steps, flip, lay) for flip in range(strata // 2, strata)]
    args = (user_factors, item_factors, ratings, user_tile, item_tile, live_count)
    return lax.switch(partner[0] - strata // 2, branches, *args)


def solution(mesh):
    split = P(("stratum", "replica"), None)
    return jax.shard_map(
        local,
        mesh=mesh,
        in_specs=(
            split,
            P("stratum", None),
            P(None, ("stratum", "replica"), None, None),
            P(None, ("stratum", "replica")),
            P(None, ("stratum", "replica")),
            P(None, ("stratum", "replica")),
            P(),
        ),
        out_specs=(split, P("stratum", None)),
        check_vma=False,
    )
```

time: 135 us -> 117 us (0.87)
  the two profiles are of different devices: /device:TPU:20 before, /device:TPU:8 now
where the time goes in v1:
time: 117 us; the launch traced here: 118 us
  starting transfers between devices  40 us (34%)
  waiting for transfers between devices  39.6 us (34%)
  Pallas kernels  36 us (31%)
  between operations  1.51 us (1%)
    ppermute x30, starting transfers between devices, swap(): lax.ppermute(value, axis, [(i, i ^ mask) for i in range(lax.axis_size(axi...  40 us
    ppermute x30, waiting for transfers between devices, swap(): lax.ppermute(value, axis, [(i, i ^ mask) for i in range(lax.axis_size(axi...  39.6 us
    pallas_call x4, Pallas kernels, slot_terms(): pl.pallas_call(functools.partial(slots_kernel, lay, sources, targets, lay...  25.2 us
    pallas_call x2, Pallas kernels, user_step(): pl.pallas_call(functools.partial(user_kernel, lay, epoch, last), out_shap...  5.21 us
    pallas_call x1, Pallas kernels, prepare(): pl.pallas_call(functools.partial(prepare_kernel, lay, epochs), out_shape=...  3.73 us
  transfers between devices with their start and end apart: 30, of which 18 were waited for; matrix products, arithmetic and copies ran while one was open for 0% of the time, Pallas kernels for 21%

profile of v1, /device:TPU:8, one launch (start us, length us, event | category | flops | bytes accessed | tf_op | source)
XLA Modules:
  0.0 118.1 jit_solution(12073069428873050361)
XLA Ops:
  1.3 116.6 %conditional.1 = (f32[4096,128]{1,0:T(8,128)}, f32[4096,128]{1,0:T(8,128)}) conditional(s32[]{:T(128)} %bitcast.8, (s32[2,1]{0,1:T(1,128)}, s32[2,256]{1,0:T(2,128)}, s32[2,256]{1,0:T(2,128)}, f32[4096,128]{1,0:T(8,128)}, s32[3]{0:T(128)S(1)}, /*index=5*/bf16[2,256,128,128]{3,2,1,0:T(8,128)(2,1)}, ...), branch_computations={%region_0.0_spmd, %region_1.0_spmd, %region_2.0_spmd, %region_3.0_... | conditional | flops 25770196992 | bytes 73221640 | solution.py:490
  1.6 3.7 %prepare.6 = (s32[80,128]{1,0:T(8,128)S(1)}, bf16[33,128,128]{2,1,0:T(8,128)(2,1)S(1)}, bf16[33,128,128]{2,1,0:T(8,128)(2,1)S(1)}) custom-call(s32[2,256]{1,0:T(2,128)} %get-tuple-element.152.user_ref, s32[2,256]{1,0:T(2,128)} %get-tuple-element.153.item_ref, s32[1,2]{1,0:T(1,128)} %bitcast.12, f32[4096,128]{1,0:T(8,128)} %get-tuple-element.155.rows_hbm.rows_ref), custom_call_target="tpu_custom_call" | custom-call | tf_op jit(solution)/shard_map/cond/branch_2_fun/prepare/pallas_call | solution.py:172
  5.3 6.2 %slots.25 = (f32[33,128,128]{2,1,0:T(8,128)S(1)}, f32[520,128]{1,0:T(8,128)S(1)}, f32[520,128]{1,0:T(8,128)S(1)}, f32[520,128]{1,0:T(8,128)S(1)}, f32[520,128]{1,0:T(8,128)S(1)}) custom-call(s32[80,128]{1,0:T(8,128)S(1)} %get-tuple-element.156.table_ref, s32[1]{0:T(128)} %bitcast.5.me_ref, s32[3]{0:T(128)S(1)} %copy-done.22, ...), custom_call_target="tpu_custom_call" | custom-call | flops 6442450944 | bytes 4194304 | tf_op jit(solution)/shard_map/cond/branch_2_fun/slots/pallas_call | solution.py:313
  11.5 3.4 %collective-permute-start.67 = (f32[520,128]{1,0:T(8,128)S(1)}, f32[520,128]{1,0:T(8,128)S(1)}, u32[]{:S(2)}, u32[]{:S(2)}) collective-permute-start(f32[520,128]{1,0:T(8,128)S(1)} %get-tuple-element.176), channel_id=1, source_target_pairs={{0,1},{1,0},{2,3},{3,2},{4,5},{5,4},{6,7},{7,6},{8,9},{9,8},{10,11... | collective-permute-start | bytes 798728 | tf_op jit(solution)/shard_map/cond/branch_2_fun/ppermute | solution.py:425
  16.5 6.4 %slots.24 = (f32[33,128,128]{2,1,0:T(8,128)S(1)}, f32[520,128]{1,0:T(8,128)S(1)}, f32[520,128]{1,0:T(8,128)S(1)}, f32[520,128]{1,0:T(8,128)S(1)}, f32[520,128]{1,0:T(8,128)S(1)}) custom-call(s32[80,128]{1,0:T(8,128)S(1)} %get-tuple-element.156.table_ref, s32[1]{0:T(128)} %bitcast.5.me_ref, s32[3]{0:T(128)S(1)} %get-tuple-element.157.where_ref, ...), custom_call_target="tpu_custom_call" | custom-call | flops 6442450944 | bytes 4194304 | tf_op jit(solution)/shard_map/cond/branch_2_fun/slots/pallas_call | solution.py:313
  22.9 4.2 %collective-permute-start.60 = (f32[520,128]{1,0:T(8,128)S(1)}, f32[520,128]{1,0:T(8,128)S(1)}, u32[]{:S(2)}, u32[]{:S(2)}) collective-permute-start(f32[520,128]{1,0:T(8,128)S(1)} %get-tuple-element.170), channel_id=1, source_target_pairs={{0,1},{1,0},{2,3},{3,2},{4,5},{5,4},{6,7},{7,6},{8,9},{9,8},{10,11... | collective-permute-start | bytes 798728 | tf_op jit(solution)/shard_map/cond/branch_2_fun/ppermute | solution.py:425
  30.4 2.9 %collective-permute-done.60.refs_1_ = f32[520,128]{1,0:T(8,128)S(1)} collective-permute-done((f32[520,128]{1,0:T(8,128)S(1)}, f32[520,128]{1,0:T(8,128)S(1)}, u32[]{:S(2)}, u32[]{:S(2)}) %collective-permute-start.60) | collective-permute-done | bytes 266272 | tf_op jit(solution)/shard_map/cond/branch_2_fun/ppermute | solution.py:425
  33.3 7.7 %collective-permute-done.61.refs_2_ = f32[520,128]{1,0:T(8,128)S(1)} collective-permute-done((f32[520,128]{1,0:T(8,128)S(1)}, f32[520,128]{1,0:T(8,128)S(1)}, u32[]{:S(2)}, u32[]{:S(2)}) %collective-permute-start.61) | collective-permute-done | bytes 266272 | tf_op jit(solution)/shard_map/cond/branch_2_fun/ppermute | solution.py:425
  41.2 1.9 %collective-permute-done.70.refs_0_.old_ref = f32[512,128]{1,0:T(8,128)S(1)} collective-permute-done((f32[512,128]{1,0:T(8,128)S(1)}, f32[512,128]{1,0:T(8,128)S(1)}, u32[]{:S(2)}, u32[]{:S(2)}) %collective-permute-start.70) | collective-permute-done | bytes 262176 | tf_op jit(solution)/shard_map/cond/branch_2_fun/ppermute | solution.py:425
  43.1 7.2 %collective-permute-start.73 = (f32[512,128]{1,0:T(8,128)S(1)}, f32[512,128]{1,0:T(8,128)S(1)}, u32[]{:S(2)}, u32[]{:S(2)}) collective-permute-start(f32[512,128]{1,0:T(8,128)S(1)} %collective-permute-done.70.refs_0_.old_ref), channel_id=1, source_target_pairs={{0,3},{1,2},{2,1},{3,0},{4,7},{5,6},{6,5},{7,4},{8,11},{9,10},{10,... | collective-permute-start | bytes 786440 | tf_op jit(solution)/shard_map/cond/branch_2_fun/ppermute | solution.py:425
  50.9 2.3 %users.12 = (f32[4096,128]{1,0:T(8,128)S(1)}, bf16[33,128,128]{2,1,0:T(8,128)(2,1)S(1)}, bf16[33,128,128]{2,1,0:T(8,128)(2,1)S(1)}) custom-call(s32[80,128]{1,0:T(8,128)S(1)} %get-tuple-element.156.table_ref, f32[4096,128]{1,0:T(8,128)S(1)} %copy-done.2, f32[33,128,128]{2,1,0:T(8,128)S(1)} %get-tuple-element.162.refs_0_, ...), custom_call_target="tpu_custom_call" | custom-call | tf_op jit(solution)/shard_map/cond/branch_2_fun/users/pallas_call | solution.py:358
  58.1 5.1 %collective-permute-done.72.refs_2_ = f32[512,128]{1,0:T(8,128)S(1)} collective-permute-done((f32[512,128]{1,0:T(8,128)S(1)}, f32[512,128]{1,0:T(8,128)S(1)}, u32[]{:S(2)}, u32[]{:S(2)}) %collective-permute-start.72) | collective-permute-done | bytes 262176 | tf_op jit(solution)/shard_map/cond/branch_2_fun/ppermute | solution.py:425
  63.6 6.3 %slots.27 = (f32[33,128,128]{2,1,0:T(8,128)S(1)}, f32[528,128]{1,0:T(8,128)S(1)}, f32[528,128]{1,0:T(8,128)S(1)}, f32[528,128]{1,0:T(8,128)S(1)}, f32[528,128]{1,0:T(8,128)S(1)}) custom-call(s32[80,128]{1,0:T(8,128)S(1)} %get-tuple-element.156.table_ref, s32[1]{0:T(128)} %bitcast.5.me_ref, s32[3]{0:T(128)S(1)} %copy-done.14, ...), custom_call_target="tpu_custom_call" | custom-call | flops 6442450944 | bytes 4194304 | tf_op jit(solution)/shard_map/cond/branch_2_fun/slots/pallas_call | solution.py:313
  69.9 3.9 %collective-permute-start.82 = (f32[528,128]{1,0:T(8,128)S(1)}, f32[528,128]{1,0:T(8,128)S(1)}, u32[]{:S(2)}, u32[]{:S(2)}) collective-permute-start(f32[528,128]{1,0:T(8,128)S(1)} %get-tuple-element.185), channel_id=1, source_target_pairs={{0,1},{1,0},{2,3},{3,2},{4,5},{5,4},{6,7},{7,6},{8,9},{9,8},{10,11... | collective-permute-start | bytes 811016 | tf_op jit(solution)/shard_map/cond/branch_2_fun/ppermute | solution.py:425
  73.9 6.3 %slots.26 = (f32[33,128,128]{2,1,0:T(8,128)S(1)}, f32[528,128]{1,0:T(8,128)S(1)}, f32[528,128]{1,0:T(8,128)S(1)}, f32[528,128]{1,0:T(8,128)S(1)}, f32[528,128]{1,0:T(8,128)S(1)}) custom-call(s32[80,128]{1,0:T(8,128)S(1)} %get-tuple-element.156.table_ref, s32[1]{0:T(128)} %bitcast.5.me_ref, s32[3]{0:T(128)S(1)} %copy-done.18, ...), custom_call_target="tpu_custom_call" | custom-call | flops 6442450944 | bytes 4194304 | tf_op jit(solution)/shard_map/cond/branch_2_fun/slots/pallas_call | solution.py:313
  80.2 4.5 %collective-permute-start.74 = (f32[528,128]{1,0:T(8,128)S(1)}, f32[528,128]{1,0:T(8,128)S(1)}, u32[]{:S(2)}, u32[]{:S(2)}) collective-permute-start(f32[528,128]{1,0:T(8,128)S(1)} %get-tuple-element.181), channel_id=1, source_target_pairs={{0,1},{1,0},{2,3},{3,2},{4,5},{5,4},{6,7},{7,6},{8,9},{9,8},{10,11... | collective-permute-start | bytes 811016 | tf_op jit(solution)/shard_map/cond/branch_2_fun/ppermute | solution.py:425
  84.7 2.1 %collective-permute-start.83 = (f32[264,128]{1,0:T(8,128)S(1)}, f32[264,128]{1,0:T(8,128)S(1)}, u32[]{:S(2)}, u32[]{:S(2)}) collective-permute-start(f32[264,128]{1,0:T(8,128)S(1)} %slice_add_fusion.9), channel_id=1, source_target_pairs={{0,2},{1,3},{2,0},{3,1},{4,6},{5,7},{6,4},{7,5},{8,10},{9,11},{10,... | collective-permute-start | bytes 405512 | tf_op jit(solution)/shard_map/cond/branch_2_fun/ppermute | solution.py:425
  86.9 5.0 %collective-permute-done.74.refs_1_ = f32[528,128]{1,0:T(8,128)S(1)} collective-permute-done((f32[528,128]{1,0:T(8,128)S(1)}, f32[528,128]{1,0:T(8,128)S(1)}, u32[]{:S(2)}, u32[]{:S(2)}) %collective-permute-start.74) | collective-permute-done | bytes 270368 | tf_op jit(solution)/shard_map/cond/branch_2_fun/ppermute | solution.py:425
  94.2 2.7 %collective-permute-done.83.refs_2_ = f32[264,128]{1,0:T(8,128)S(1)} collective-permute-done((f32[264,128]{1,0:T(8,128)S(1)}, f32[264,128]{1,0:T(8,128)S(1)}, u32[]{:S(2)}, u32[]{:S(2)}) %collective-permute-start.83) | collective-permute-done | bytes 135200 | tf_op jit(solution)/shard_map/cond/branch_2_fun/ppermute | solution.py:425
  97.8 2.0 %collective-permute-done.75.refs_2_ = f32[264,128]{1,0:T(8,128)S(1)} collective-permute-done((f32[264,128]{1,0:T(8,128)S(1)}, f32[264,128]{1,0:T(8,128)S(1)}, u32[]{:S(2)}, u32[]{:S(2)}) %collective-permute-start.75) | collective-permute-done | bytes 135200 | tf_op jit(solution)/shard_map/cond/branch_2_fun/ppermute | solution.py:425
  103.5 1.9 %collective-permute-start.89 = (f32[512,128]{1,0:T(8,128)S(1)}, f32[512,128]{1,0:T(8,128)S(1)}, u32[]{:S(2)}, u32[]{:S(2)}) collective-permute-start(f32[512,128]{1,0:T(8,128)S(1)} %pad_maximum_fusion.11.refs_6_), channel_id=1, source_target_pairs={{0,2},{1,3},{2,0},{3,1},{4,6},{5,7},{6,4},{7,5},{8,10},{9,11},{10,... | collective-permute-start | bytes 786440 | tf_op jit(solution)/shard_map/cond/branch_2_fun/ppermute | solution.py:425
  106.5 2.1 %collective-permute-start.81 = (f32[512,128]{1,0:T(8,128)S(1)}, f32[512,128]{1,0:T(8,128)S(1)}, u32[]{:S(2)}, u32[]{:S(2)}) collective-permute-start(f32[512,128]{1,0:T(8,128)S(1)} %pad_maximum_fusion.9.refs_2_), channel_id=1, source_target_pairs={{0,2},{1,3},{2,0},{3,1},{4,6},{5,7},{6,4},{7,5},{8,10},{9,11},{10,... | collective-permute-start | bytes 786440 | tf_op jit(solution)/shard_map/cond/branch_2_fun/ppermute | solution.py:425
  108.6 2.9 %users.13 = f32[4096,128]{1,0:T(8,128)} custom-call(s32[80,128]{1,0:T(8,128)S(1)} %get-tuple-element.156.table_ref, f32[4096,128]{1,0:T(8,128)S(1)} %get-tuple-element.165.rows_ref, f32[33,128,128]{2,1,0:T(8,128)S(1)} %get-tuple-element.173.refs_0_, f32[33,128,128]{2,1,0:T(8,128)S(1)} %get-tuple-element.179.refs_1_), custom_call_target="tpu_custom_call" | custom-call | tf_op jit(solution)/shard_map/cond/branch_2_fun/users/pallas_call | solution.py:358
  112.8 3.4 %collective-permute-done.77.refs_1_ = f32[512,128]{1,0:T(8,128)S(1)} collective-permute-done((f32[512,128]{1,0:T(8,128)S(1)}, f32[512,128]{1,0:T(8,128)S(1)}, u32[]{:S(2)}, u32[]{:S(2)}) %collective-permute-start.77) | collective-permute-done | bytes 262176 | tf_op jit(solution)/shard_map/cond/branch_2_fun/ppermute | solution.py:425
  (72 shorter events, 21.7 us)
Async XLA Ops:
  11.5 15.6 %collective-permute-start.67 = (f32[520,128]{1,0:T(8,128)S(1)}, f32[520,128]{1,0:T(8,128)S(1)}, u32[]{:S(2)}, u32[]{:S(2)}) collective-permute-start(f32[520,128]{1,0:T(8,128)S(1)} %get-tuple-element.176), channel_id=1, source_target_pairs={{0,1},{1,0},{2,3},{3,2},{4,5},{5,4},{6,7},{7,6},{8,9},{9,8},{10,11... | collective-permute-start | bytes 798728 | tf_op jit(solution)/shard_map/cond/branch_2_fun/ppermute | solution.py:425
  15.0 14.5 %collective-permute-start.68 = (f32[520,128]{1,0:T(8,128)S(1)}, f32[520,128]{1,0:T(8,128)S(1)}, u32[]{:S(2)}, u32[]{:S(2)}) collective-permute-start(f32[520,128]{1,0:T(8,128)S(1)} %get-tuple-element.177), channel_id=1, source_target_pairs={{0,2},{1,3},{2,0},{3,1},{4,6},{5,7},{6,4},{7,5},{8,10},{9,11},{10,... | collective-permute-start | bytes 798728 | tf_op jit(solution)/shard_map/cond/branch_2_fun/ppermute | solution.py:425
  15.0 14.4 %collective-permute-start.69 = (f32[520,128]{1,0:T(8,128)S(1)}, f32[520,128]{1,0:T(8,128)S(1)}, u32[]{:S(2)}, u32[]{:S(2)}) collective-permute-start(f32[520,128]{1,0:T(8,128)S(1)} %get-tuple-element.178), channel_id=1, source_target_pairs={{0,3},{1,2},{2,1},{3,0},{4,7},{5,6},{6,5},{7,4},{8,11},{9,10},{10,... | collective-permute-start | bytes 798728 | tf_op jit(solution)/shard_map/cond/branch_2_fun/ppermute | solution.py:425
  22.9 10.4 %collective-permute-start.60 = (f32[520,128]{1,0:T(8,128)S(1)}, f32[520,128]{1,0:T(8,128)S(1)}, u32[]{:S(2)}, u32[]{:S(2)}) collective-permute-start(f32[520,128]{1,0:T(8,128)S(1)} %get-tuple-element.170), channel_id=1, source_target_pairs={{0,1},{1,0},{2,3},{3,2},{4,5},{5,4},{6,7},{7,6},{8,9},{9,8},{10,11... | collective-permute-start | bytes 798728 | tf_op jit(solution)/shard_map/cond/branch_2_fun/ppermute | solution.py:425
  27.1 13.9 %collective-permute-start.61 = (f32[520,128]{1,0:T(8,128)S(1)}, f32[520,128]{1,0:T(8,128)S(1)}, u32[]{:S(2)}, u32[]{:S(2)}) collective-permute-start(f32[520,128]{1,0:T(8,128)S(1)} %get-tuple-element.171), channel_id=1, source_target_pairs={{0,2},{1,3},{2,0},{3,1},{4,6},{5,7},{6,4},{7,5},{8,10},{9,11},{10,... | collective-permute-start | bytes 798728 | tf_op jit(solution)/shard_map/cond/branch_2_fun/ppermute | solution.py:425
  27.1 13.9 %collective-permute-start.62 = (f32[520,128]{1,0:T(8,128)S(1)}, f32[520,128]{1,0:T(8,128)S(1)}, u32[]{:S(2)}, u32[]{:S(2)}) collective-permute-start(f32[520,128]{1,0:T(8,128)S(1)} %get-tuple-element.172), channel_id=1, source_target_pairs={{0,3},{1,2},{2,1},{3,0},{4,7},{5,6},{6,5},{7,4},{8,11},{9,10},{10,... | collective-permute-start | bytes 798728 | tf_op jit(solution)/shard_map/cond/branch_2_fun/ppermute | solution.py:425
  29.6 13.6 %collective-permute-start.70 = (f32[512,128]{1,0:T(8,128)S(1)}, f32[512,128]{1,0:T(8,128)S(1)}, u32[]{:S(2)}, u32[]{:S(2)}) collective-permute-start(f32[512,128]{1,0:T(8,128)S(1)} %items.37), channel_id=1, source_target_pairs={{0,24},{4,28},{8,16},{12,20},{16,8},{20,12},{24,0},{28,4},{1,25},{... | collective-permute-start | bytes 786440 | tf_op jit(solution)/shard_map/cond/branch_2_fun/ppermute | solution.py:425
  41.1 13.5 %collective-permute-start.63 = (f32[512,128]{1,0:T(8,128)S(1)}, f32[512,128]{1,0:T(8,128)S(1)}, u32[]{:S(2)}, u32[]{:S(2)}) collective-permute-start(f32[512,128]{1,0:T(8,128)S(1)} %items.36), channel_id=1, source_target_pairs={{0,24},{4,28},{8,16},{12,20},{16,8},{20,12},{24,0},{28,4},{1,25},{... | collective-permute-start | bytes 786440 | tf_op jit(solution)/shard_map/cond/branch_2_fun/ppermute | solution.py:425
  43.1 14.3 %collective-permute-start.73 = (f32[512,128]{1,0:T(8,128)S(1)}, f32[512,128]{1,0:T(8,128)S(1)}, u32[]{:S(2)}, u32[]{:S(2)}) collective-permute-start(f32[512,128]{1,0:T(8,128)S(1)} %collective-permute-done.70.refs_0_.old_ref), channel_id=1, source_target_pairs={{0,3},{1,2},{2,1},{3,0},{4,7},{5,6},{6,5},{7,4},{8,11},{9,10},{10,... | collective-permute-start | bytes 786440 | tf_op jit(solution)/shard_map/cond/branch_2_fun/ppermute | solution.py:425
  50.3 12.8 %collective-permute-start.72 = (f32[512,128]{1,0:T(8,128)S(1)}, f32[512,128]{1,0:T(8,128)S(1)}, u32[]{:S(2)}, u32[]{:S(2)}) collective-permute-start(f32[512,128]{1,0:T(8,128)S(1)} %collective-permute-done.70.refs_0_.old_ref), channel_id=1, source_target_pairs={{0,2},{1,3},{2,0},{3,1},{4,6},{5,7},{6,4},{7,5},{8,10},{9,11},{10,... | collective-permute-start | bytes 786440 | tf_op jit(solution)/shard_map/cond/branch_2_fun/ppermute | solution.py:425
  50.3 13.3 %collective-permute-start.71 = (f32[512,128]{1,0:T(8,128)S(1)}, f32[512,128]{1,0:T(8,128)S(1)}, u32[]{:S(2)}, u32[]{:S(2)}) collective-permute-start(f32[512,128]{1,0:T(8,128)S(1)} %collective-permute-done.70.refs_0_.old_ref), channel_id=1, source_target_pairs={{0,1},{1,0},{2,3},{3,2},{4,5},{5,4},{6,7},{7,6},{8,9},{9,8},{10,11... | collective-permute-start | bytes 786440 | tf_op jit(solution)/shard_map/cond/branch_2_fun/ppermute | solution.py:425
  54.6 19.3 %collective-permute-start.66 = (f32[512,128]{1,0:T(8,128)S(1)}, f32[512,128]{1,0:T(8,128)S(1)}, u32[]{:S(2)}, u32[]{:S(2)}) collective-permute-start(f32[512,128]{1,0:T(8,128)S(1)} %collective-permute-done.63.refs_0_.old_ref), channel_id=1, source_target_pairs={{0,3},{1,2},{2,1},{3,0},{4,7},{5,6},{6,5},{7,4},{8,11},{9,10},{10,... | collective-permute-start | bytes 786440 | tf_op jit(solution)/shard_map/cond/branch_2_fun/ppermute | solution.py:425
  56.2 17.7 %collective-permute-start.65 = (f32[512,128]{1,0:T(8,128)S(1)}, f32[512,128]{1,0:T(8,128)S(1)}, u32[]{:S(2)}, u32[]{:S(2)}) collective-permute-start(f32[512,128]{1,0:T(8,128)S(1)} %collective-permute-done.63.refs_0_.old_ref), channel_id=1, source_target_pairs={{0,2},{1,3},{2,0},{3,1},{4,6},{5,7},{6,4},{7,5},{8,10},{9,11},{10,... | collective-permute-start | bytes 786440 | tf_op jit(solution)/shard_map/cond/branch_2_fun/ppermute | solution.py:425
  57.5 16.4 %collective-permute-start.64 = (f32[512,128]{1,0:T(8,128)S(1)}, f32[512,128]{1,0:T(8,128)S(1)}, u32[]{:S(2)}, u32[]{:S(2)}) collective-permute-start(f32[512,128]{1,0:T(8,128)S(1)} %collective-permute-done.63.refs_0_.old_ref), channel_id=1, source_target_pairs={{0,1},{1,0},{2,3},{3,2},{4,5},{5,4},{6,7},{7,6},{8,9},{9,8},{10,11... | collective-permute-start | bytes 786440 | tf_op jit(solution)/shard_map/cond/branch_2_fun/ppermute | solution.py:425
  69.9 14.8 %collective-permute-start.82 = (f32[528,128]{1,0:T(8,128)S(1)}, f32[528,128]{1,0:T(8,128)S(1)}, u32[]{:S(2)}, u32[]{:S(2)}) collective-permute-start(f32[528,128]{1,0:T(8,128)S(1)} %get-tuple-element.185), channel_id=1, source_target_pairs={{0,1},{1,0},{2,3},{3,2},{4,5},{5,4},{6,7},{7,6},{8,9},{9,8},{10,11... | collective-permute-start | bytes 811016 | tf_op jit(solution)/shard_map/cond/branch_2_fun/ppermute | solution.py:425
  73.8 13.0 %collective-permute-start.86 = (f32[528,128]{1,0:T(8,128)S(1)}, f32[528,128]{1,0:T(8,128)S(1)}, u32[]{:S(2)}, u32[]{:S(2)}) collective-permute-start(f32[528,128]{1,0:T(8,128)S(1)} %get-tuple-element.187), channel_id=1, source_target_pairs={{0,2},{1,3},{2,0},{3,1},{4,6},{5,7},{6,4},{7,5},{8,10},{9,11},{10,... | collective-permute-start | bytes 811016 | tf_op jit(solution)/shard_map/cond/branch_2_fun/ppermute | solution.py:425
  80.2 11.8 %collective-permute-start.74 = (f32[528,128]{1,0:T(8,128)S(1)}, f32[528,128]{1,0:T(8,128)S(1)}, u32[]{:S(2)}, u32[]{:S(2)}) collective-permute-start(f32[528,128]{1,0:T(8,128)S(1)} %get-tuple-element.181), channel_id=1, source_target_pairs={{0,1},{1,0},{2,3},{3,2},{4,5},{5,4},{6,7},{7,6},{8,9},{9,8},{10,11... | collective-permute-start | bytes 811016 | tf_op jit(solution)/shard_map/cond/branch_2_fun/ppermute | solution.py:425
  84.7 9.3 %collective-permute-start.78 = (f32[528,128]{1,0:T(8,128)S(1)}, f32[528,128]{1,0:T(8,128)S(1)}, u32[]{:S(2)}, u32[]{:S(2)}) collective-permute-start(f32[528,128]{1,0:T(8,128)S(1)} %get-tuple-element.183), channel_id=1, source_target_pairs={{0,2},{1,3},{2,0},{3,1},{4,6},{5,7},{6,4},{7,5},{8,10},{9,11},{10,... | collective-permute-start | bytes 811016 | tf_op jit(solution)/shard_map/cond/branch_2_fun/ppermute | solution.py:425
  84.7 12.2 %collective-permute-start.83 = (f32[264,128]{1,0:T(8,128)S(1)}, f32[264,128]{1,0:T(8,128)S(1)}, u32[]{:S(2)}, u32[]{:S(2)}) collective-permute-start(f32[264,128]{1,0:T(8,128)S(1)} %slice_add_fusion.9), channel_id=1, source_target_pairs={{0,2},{1,3},{2,0},{3,1},{4,6},{5,7},{6,4},{7,5},{8,10},{9,11},{10,... | collective-permute-start | bytes 405512 | tf_op jit(solution)/shard_map/cond/branch_2_fun/ppermute | solution.py:425
  86.8 10.2 %collective-permute-start.87 = (f32[264,128]{1,0:T(8,128)S(1)}, f32[264,128]{1,0:T(8,128)S(1)}, u32[]{:S(2)}, u32[]{:S(2)}) collective-permute-start(f32[264,128]{1,0:T(8,128)S(1)} %slice_add_fusion.8), channel_id=1, source_target_pairs={{0,1},{1,0},{2,3},{3,2},{4,5},{5,4},{6,7},{7,6},{8,9},{9,8},{10,11... | collective-permute-start | bytes 405512 | tf_op jit(solution)/shard_map/cond/branch_2_fun/ppermute | solution.py:425
  103.0 9.3 %collective-permute-start.85 = (f32[512,128]{1,0:T(8,128)S(1)}, f32[512,128]{1,0:T(8,128)S(1)}, u32[]{:S(2)}, u32[]{:S(2)}) collective-permute-start(f32[512,128]{1,0:T(8,128)S(1)} %pad_maximum_fusion.10.refs_4_), channel_id=1, source_target_pairs={{0,1},{1,0},{2,3},{3,2},{4,5},{5,4},{6,7},{7,6},{8,9},{9,8},{10,11... | collective-permute-start | bytes 786440 | tf_op jit(solution)/shard_map/cond/branch_2_fun/ppermute | solution.py:425
  103.5 9.3 %collective-permute-start.89 = (f32[512,128]{1,0:T(8,128)S(1)}, f32[512,128]{1,0:T(8,128)S(1)}, u32[]{:S(2)}, u32[]{:S(2)}) collective-permute-start(f32[512,128]{1,0:T(8,128)S(1)} %pad_maximum_fusion.11.refs_6_), channel_id=1, source_target_pairs={{0,2},{1,3},{2,0},{3,1},{4,6},{5,7},{6,4},{7,5},{8,10},{9,11},{10,... | collective-permute-start | bytes 786440 | tf_op jit(solution)/shard_map/cond/branch_2_fun/ppermute | solution.py:425
  106.3 9.9 %collective-permute-start.77 = (f32[512,128]{1,0:T(8,128)S(1)}, f32[512,128]{1,0:T(8,128)S(1)}, u32[]{:S(2)}, u32[]{:S(2)}) collective-permute-start(f32[512,128]{1,0:T(8,128)S(1)} %pad_maximum_fusion.8.refs_0_), channel_id=1, source_target_pairs={{0,1},{1,0},{2,3},{3,2},{4,5},{5,4},{6,7},{7,6},{8,9},{9,8},{10,11... | collective-permute-start | bytes 786440 | tf_op jit(solution)/shard_map/cond/branch_2_fun/ppermute | solution.py:425
  106.5 9.7 %collective-permute-start.81 = (f32[512,128]{1,0:T(8,128)S(1)}, f32[512,128]{1,0:T(8,128)S(1)}, u32[]{:S(2)}, u32[]{:S(2)}) collective-permute-start(f32[512,128]{1,0:T(8,128)S(1)} %pad_maximum_fusion.9.refs_2_), channel_id=1, source_target_pairs={{0,2},{1,3},{2,0},{3,1},{4,6},{5,7},{6,4},{7,5},{8,10},{9,11},{10,... | collective-permute-start | bytes 786440 | tf_op jit(solution)/shard_map/cond/branch_2_fun/ppermute | solution.py:425
  (12 other events, 109.0 us)

commit v2 on v1

--- a/solution.py
+++ b/solution.py
@@ -13,7 +13,7 @@
 
 TILE = 128
 SPLIT = (1, 1)
-LANES = (1, 2)
+LANES = ((1, 1), (2, 2))
 DIRECT_SUM = ((1, 1), (0, 0))
 DIRECT_SPREAD = ((1, 1), (0, 0))
 UNITS = 8
@@ -37,14 +37,14 @@
 
 
 class Lane:
-    def __init__(self, chunk_first, share, lane, lanes, replicas):
+    def __init__(self, chunk_first, share, lane, lanes, replicas, turn):
         self.chunk_first, self.share, self.replicas = chunk_first, share, replicas
         self.tiles = share // lanes
         self.skip = lane * self.tiles
         self.rows = self.tiles * TILE
         self.sent = self.rows + COUNT_ROWS
         levels = replicas.bit_length() - 1
-        self.bits = [1 << (lane + i) % levels for i in range(levels)]
+        self.bits = [1 << (lane + turn + i) % levels for i in range(levels)]
 
     def arrays(self, direct):
         if direct:
@@ -67,29 +67,29 @@
             self.lanes.append([])
             for c in range(self.chunks):
                 share = self.tiles[c] // replicas
-                lanes = wanted if share % wanted == 0 else 1
-                self.lanes[-1].append([Lane(self.firsts[c], share, n, lanes, replicas) for n in range(lanes)])
+                lanes = wanted[c] if share % wanted[c] == 0 else 1
+                self.lanes[-1].append([Lane(self.firsts[c], share, n, lanes, replicas, c) for n in range(lanes)])
         self.groups = self.chunks * users
         self.group_cols = up(self.groups + 1, 128)
-        self.steps = up((slots + self.groups) // STEP + self.chunks + AHEAD + 1, 8)
-        self.start_at = self.steps
-        self.count_at = self.start_at + self.group_cols // 128
-        self.seen_at = self.count_at + 1
-        self.table_rows = up(self.seen_at + 1, 8)
-
-    def start(self, table_ref, epoch, chunk):
-        at = chunk * self.users
-        row = lax.shift_right_logical(at, 7)
-        return table_ref[epoch * self.table_rows + self.start_at + row, lax.bitwise_and(at, 127)]
+        self.depth = up(slots + users, STEP) // STEP
+        self.info_at = self.depth + AHEAD
+        self.seen_at = self.info_at + 1
+        self.count_at = self.info_at + 2
+        self.table_rows = up(self.info_at + 3, 8)
+
+
+ME, EPOCH, STEPS, FIRST = range(4)
 
 
 def column(row, across):
-    return jnp.broadcast_to(row, (across, row.shape[1])).T
+    one = jnp.broadcast_to(row, (128, row.shape[1])).T
+    return jnp.concatenate([one] * (across // 128), axis=1)
 
 
 def low_tiles(rows, low_ref, lowt_ref, a):
-    low_ref[a] = rows.astype(jnp.bfloat16)
-    lowt_ref[a] = rows.T.astype(jnp.bfloat16)
+    low = rows.astype(jnp.bfloat16)
+    low_ref[a] = low
+    lowt_ref[a] = low.T
 
 
 def slot_table(lay, user, item, live):
@@ -109,26 +109,26 @@
     count = total(column(group, groups) == iota((n, groups), 1))
     padded = column((count + 1) // 2 * 2, groups)
     above, here = iota((groups, groups), 0), iota((groups, groups), 1)
-    inside = total((above < here) & (above // users == here // users), padded)
-    steps = (total(above // users == here // users, padded) + STEP - 1) // STEP
-    start = total((above % users == 0) & (above // users < here // users), column(steps, groups))
-    base = start * STEP + inside
+    kin = above // users == here // users
+    inside = total((above < here) & kin, padded)
+    steps = (total(kin, padded) + STEP - 1) // STEP
+    every = iota((1, groups), 1)
+    base = every // users * (lay.depth * STEP) + inside
     place = rank + total(iota((groups, n), 0) == group, column(base, n))
     place = jnp.where(live, place, -1)
-    every = iota((1, groups), 1)
     spare = jnp.where((count % 2 == 1) & (every < lay.groups), base + count, -1)
     pad = sum(jnp.where(every // users == c, tiles, 0) for c, tiles in enumerate(lay.tiles))
-    cols = lay.steps * STEP
-    cols = up(cols, 128)
+    cols = up(lay.chunks * lay.depth * STEP, 128)
     order = total(column(place, cols) == iota((n, cols), 1), column(packed - users, cols))
     order += total(column(spare, cols) == iota((groups, cols), 1), column(every % users - users + (pad << FIELD), cols))
     order += users
     seen_user = total(column(jnp.where(live, user, -1), 128) == iota((n, 128), 1))
     seen_item = total(column(jnp.where(live, item, -1), 128) == iota((n, 128), 1))
-    return order, start, seen_user, seen_item
-
-
-def prepare_kernel(lay, epochs, user_ref, item_ref, live_ref, rows_hbm, table_ref, low_ref, lowt_ref, rows_ref, sems):
+    return order, steps, seen_user, seen_item
+
+
+def prepare_kernel(lay, epochs, me_ref, user_ref, item_ref, live_ref, rows_hbm, *refs):
+    tables, (low_ref, lowt_ref, rows_ref, sems) = refs[:-4], refs[-4:]
     parts = sems.shape[0]
     height = rows_ref.shape[0] // parts
     copies = []
@@ -136,18 +136,28 @@
         at = pl.ds(p * height, height)
         copies.append(pltpu.make_async_copy(rows_hbm.at[at, :], rows_ref.at[at, :], sems.at[p]))
         copies[-1].start()
+    lane = lax.broadcasted_iota(jnp.int32, (lay.table_rows, 128), 1)
+    mask = (1 << FIELD) - 1
     for e in range(epochs):
         live = lax.broadcasted_iota(jnp.int32, (1, lay.slots), 1) < live_ref[:, e : e + 1]
-        order, start, seen_user, seen_item = slot_table(lay, user_ref[e : e + 1, :], item_ref[e : e + 1, :], live)
-        top = e * lay.table_rows
-        mask = (1 << FIELD) - 1
-        for at, values in ((0, order >> 2 * FIELD), (STEP, order & mask), (2 * STEP, (order >> FIELD) & mask)):
-            for g in range(lay.steps):
-                table_ref[top + g : top + g + 1, at : at + STEP] = values[:, g * STEP : (g + 1) * STEP]
-        for n in range(lay.group_cols // 128):
-            table_ref[top + lay.start_at + n : top + lay.start_at + n + 1, :] = start[:, n * 128 : (n + 1) * 128]
-        table_ref[top + lay.count_at : top + lay.count_at + 1, :] = seen_user
-        table_ref[top + lay.seen_at : top + lay.seen_at + 1, :] = seen_item
+        order, steps, seen_user, seen_item = slot_table(lay, user_ref[e : e + 1, :], item_ref[e : e + 1, :], live)
+        every = lax.broadcasted_iota(jnp.int32, steps.shape, 1)
+        for c in range(lay.chunks):
+            table_ref = tables[e * lay.chunks + c]
+            table_ref[...] = jnp.full(table_ref.shape, lay.users, jnp.int32)
+            for g in range(lay.depth):
+                at = (c * lay.depth + g) * STEP
+                table_ref[g : g + 1, 0:STEP] = order[:, at : at + STEP]
+            packed = table_ref[...]
+            user = pltpu.roll(packed & mask, STEP, 1)
+            item = pltpu.roll((packed >> FIELD) & mask, 2 * STEP, 1)
+            table_ref[...] = jnp.where(lane < STEP, packed >> 2 * FIELD, jnp.where(lane < 2 * STEP, user, item))
+            mine = jnp.sum(jnp.where(every == c * lay.users, steps, 0), axis=1, keepdims=True)
+            info = jnp.where(lane[:1] == STEPS, mine, lay.firsts[c])
+            info = jnp.where(lane[:1] == ME, me_ref[0], jnp.where(lane[:1] == EPOCH, e, info))
+            table_ref[lay.info_at : lay.info_at + 1, :] = info
+            table_ref[lay.seen_at : lay.seen_at + 1, :] = seen_item
+            table_ref[lay.count_at : lay.count_at + 1, :] = seen_user
     low_ref[lay.users] = jnp.zeros((TILE, TILE), jnp.bfloat16)
     lowt_ref[lay.users] = jnp.zeros((TILE, TILE), jnp.bfloat16)
     share = lay.users // parts
@@ -166,41 +176,38 @@
     return jax.ShapeDtypeStruct((lay.users + 1, TILE, TILE), jnp.bfloat16)
 
 
-def prepare(lay, user_tile, item_tile, live_count, user_rows):
+def prepare(lay, me, user_tile, item_tile, live_count, user_rows):
     epochs = user_tile.shape[0]
     parts = 4
-    return pl.pallas_call(
+    out = pl.pallas_call(
         functools.partial(prepare_kernel, lay, epochs),
-        out_shape=[
-            jax.ShapeDtypeStruct((epochs * lay.table_rows, 128), jnp.int32),
-            low_shape(lay),
-            low_shape(lay),
-        ],
-        in_specs=[VMEM, VMEM, VMEM, ANY],
-        out_specs=[VMEM] * 3,
+        out_shape=[jax.ShapeDtypeStruct((lay.table_rows, 128), jnp.int32)] * (epochs * lay.chunks)
+        + [low_shape(lay)] * 2,
+        in_specs=[SMEM, VMEM, VMEM, VMEM, ANY],
+        out_specs=[VMEM] * (epochs * lay.chunks + 2),
         scratch_shapes=[pltpu.VMEM(user_rows.shape, jnp.float32), pltpu.SemaphoreType.DMA((parts,))],
         compiler_params=PARAMS,
         name="prepare",
-    )(user_tile, item_tile, live_count, user_rows)
+    )(me, user_tile, item_tile, live_count, user_rows)
+    tables = [out[e * lay.chunks : (e + 1) * lay.chunks] for e in range(epochs)]
+    return tables, out[-2], out[-1]
 
 
 def slots_kernel(
-    lay, sources, targets, tiles, table_ref, me_ref, where_ref, ratings_ref, low_ref, lowt_ref, *refs
+    lay, sources, targets, tiles, table_ref, ratings_ref, low_ref, lowt_ref, *refs
 ):
     count_in = sum(len(arrays) for _, arrays in sources) if sources else 1
     count_out = sum(len(arrays) for _, arrays in targets)
     block_refs, refs = refs[:count_in], refs[count_in:]
     user_grad, piece_refs = refs[0], refs[1 : 1 + count_out]
     buf, sems, item_low, item_grad = refs[1 + count_out :]
-    me, epoch, chunk, chunk_first = me_ref[0], where_ref[0], where_ref[1], where_ref[2]
-    top = epoch * lay.table_rows + lay.start(table_ref, epoch, chunk)
-    steps = lay.start(table_ref, epoch, chunk + 1) - lay.start(table_ref, epoch, chunk)
+    me, epoch, steps, chunk_first = [table_ref[lay.info_at, n] for n in (ME, EPOCH, STEPS, FIRST)]
     zero = jnp.zeros((TILE, TILE), jnp.float32)
 
     def fetch(g):
         ring = lax.bitwise_and(g, RING - 1)
         for s in range(STEP):
-            slot = table_ref[top + g, s]
+            slot = table_ref[g, s]
             pltpu.make_async_copy(ratings_ref.at[epoch, slot], buf.at[ring, s], sems.at[ring]).start()
 
     def land(g):
@@ -251,8 +258,8 @@
         ring = lax.bitwise_and(g, RING - 1)
         units = []
         for n in range(UNITS):
-            user = table_ref[top + g, STEP + 2 * n]
-            items = [table_ref[top + g, 2 * STEP + 2 * n + s] for s in range(2)]
+            user = table_ref[g, STEP + 2 * n]
+            items = [table_ref[g, 2 * STEP + 2 * n + s] for s in range(2)]
             right = jnp.concatenate([item_low[b] for b in items], axis=0)
             predicted = lax.dot_general(low_ref[user], right, CONTRACT_LAST, preferred_element_type=jnp.float32)
             rating = jnp.concatenate([buf[ring, 2 * n + s] for s in range(2)], axis=1)
@@ -283,7 +290,7 @@
                 for j in range(lane.tiles):
                     at = n * lane.sent + j * TILE
                     out[at : at + TILE, :] = item_grad[first + j]
-                    seen = table_ref[epoch * lay.table_rows + lay.seen_at, chunk_first + first + j]
+                    seen = table_ref[lay.seen_at, chunk_first + first + j]
                     counts = jnp.where(row == j, seen, counts)
                 at = n * lane.sent + lane.rows
                 out[at : at + COUNT_ROWS, :] = counts.astype(jnp.float32)
@@ -299,7 +306,7 @@
     return [(lane, lane.arrays(direct[epoch][chunk])) for lane in lay.lanes[epoch][chunk]]
 
 
-def slot_terms(lay, epoch, chunk, table, me, ratings, low, lowt, blocks):
+def slot_terms(lay, epoch, chunk, table, ratings, low, lowt, blocks):
     sources = routes(lay, DIRECT_SPREAD, epoch - 1, chunk) if epoch else None
     targets = routes(lay, DIRECT_SUM, epoch, chunk)
     pieces = [
@@ -309,11 +316,10 @@
     ]
     user_grad = jax.ShapeDtypeStruct((lay.users + 1, TILE, TILE), jnp.float32)
     live = lay.slots // lay.chunks
-    where = jnp.array([epoch, chunk, lay.firsts[chunk]], jnp.int32)
     out = pl.pallas_call(
         functools.partial(slots_kernel, lay, sources, targets, lay.tiles[chunk]),
         out_shape=[user_grad] + pieces,
-        in_specs=[SMEM, SMEM, SMEM, ANY, VMEM, VMEM] + [VMEM] * len(blocks),
+        in_specs=[SMEM, ANY, VMEM, VMEM] + [VMEM] * len(blocks),
         out_specs=[VMEM] * (1 + len(pieces)),
         scratch_shapes=[
             pltpu.VMEM((RING, STEP, TILE, TILE), jnp.bfloat16),
@@ -326,16 +332,16 @@
         ),
         compiler_params=pltpu.CompilerParams(vmem_limit_bytes=SLOT_VMEM_BYTES),
         name="slots",
-    )(table, me, where, ratings, low, lowt, *blocks)
+    )(table, ratings, low, lowt, *blocks)
     parts = iter(out[1:])
     return out[0], [[next(parts) for _ in arrays] for _, arrays in targets]
 
 
-def user_kernel(lay, epoch, last, table_ref, rows_ref, *refs):
+def user_kernel(lay, last, table_ref, rows_ref, *refs):
     grads, refs = refs[: lay.chunks], refs[lay.chunks :]
 
     def one(a, _):
-        seen = table_ref[epoch * lay.table_rows + lay.count_at, a]
+        seen = table_ref[lay.count_at, a]
         seen = jnp.maximum(jnp.broadcast_to(seen, (1, TILE)).astype(jnp.float32), 1.0)
         at = pl.ds(pl.multiple_of(a * TILE, TILE), TILE)
         grad = sum(grad_ref[a] for grad_ref in grads)
@@ -351,12 +357,12 @@
         refs[2][lay.users] = jnp.zeros((TILE, TILE), jnp.bfloat16)
 
 
-def user_step(lay, epoch, last, table, rows, grads):
+def user_step(lay, last, table, rows, grads):
     out_shape = [jax.ShapeDtypeStruct(rows.shape, jnp.float32)]
     if not last:
         out_shape += [low_shape(lay)] * 2
     return pl.pallas_call(
-        functools.partial(user_kernel, lay, epoch, last),
+        functools.partial(user_kernel, lay, last),
         out_shape=out_shape,
         in_specs=[SMEM] + [VMEM] * (1 + len(grads)),
         out_specs=[VMEM] * len(out_shape),
@@ -451,20 +457,20 @@
     me = lax.axis_index("replica").astype(jnp.int32).reshape(1)
     epochs = ratings.shape[0]
     rows = user_factors
-    table, low, lowt = prepare(lay, user_tile, item_tile, live_count.T, rows)
+    tables, low, lowt = prepare(lay, me, user_tile, item_tile, live_count.T, rows)
     blocks = [[[item_factors]]] * lay.chunks
     for e in range(epochs):
         last = e + 1 == epochs
         grads, parts = [], []
         for c in range(lay.chunks):
             block = [array for arrays in blocks[c] for array in arrays]
-            grad, pieces = slot_terms(lay, e, c, table, me, ratings, low, lowt, block)
+            grad, pieces = slot_terms(lay, e, c, tables[e][c], ratings, low, lowt, block)
             grads.append(grad)
             parts.append([gather_sum(lane, DIRECT_SUM[e][c], held) for lane, held in zip(lay.lanes[e][c], pieces)])
         if last:
-            (rows,) = user_step(lay, e, last, table, rows, grads)
+            (rows,) = user_step(lay, last, tables[e][0], rows, grads)
         else:
-            rows, low, lowt = user_step(lay, e, last, table, rows, grads)
+            rows, low, lowt = user_step(lay, last, tables[e][0], rows, grads)
         fresh = []
         for c in range(lay.chunks):
             lanes = []

time: 117 us -> 111 us (0.949)
  the two profiles are of different devices: /device:TPU:8 before, /device:TPU:0 now
where the time goes in v2:
time: 111 us; the launch traced here: 113 us
  starting transfers between devices  50.3 us (45%)
  Pallas kernels  31.2 us (28%)
  waiting for transfers between devices  29.3 us (26%)
  between operations  1.5 us (1%)
    ppermute x30, starting transfers between devices, swap(): lax.ppermute(value, axis, [(i, i ^ mask) for i in range(lax.axis_size(axi...  50.3 us
    ppermute x30, waiting for transfers between devices, swap(): lax.ppermute(value, axis, [(i, i ^ mask) for i in range(lax.axis_size(axi...  29.3 us
    pallas_call x4, Pallas kernels, slot_terms(): pl.pallas_call(functools.partial(slots_kernel, lay, sources, targets, lay...  21.5 us
    pallas_call x2, Pallas kernels, user_step(): pl.pallas_call(functools.partial(user_kernel, lay, last), out_shape=out_s...  4.15 us
    pallas_call x1, Pallas kernels, prepare(): pl.pallas_call(functools.partial(prepare_kernel, lay, epochs), out_shape=...  3.68 us
  transfers between devices with their start and end apart: 30, of which 13 were waited for; matrix products, arithmetic and copies ran while one was open for 0% of the time, Pallas kernels for 18%

profile of v2, /device:TPU:0, one launch (start us, length us, event | category | flops | bytes accessed | tf_op | source)
XLA Modules:
  0.0 113.1 jit_solution(2317443240306584679)
XLA Ops:
  1.3 111.6 %conditional.1 = (f32[4096,128]{1,0:T(8,128)}, f32[4096,128]{1,0:T(8,128)}) conditional(s32[]{:T(128)} %bitcast.8, (s32[2,1]{0,1:T(1,128)}, s32[2,256]{1,0:T(2,128)}, s32[2,256]{1,0:T(2,128)}, f32[4096,128]{1,0:T(8,128)}, bf16[2,256,128,128]{3,2,1,0:T(8,128)(2,1)}, /*index=5*/f32[4096,128]{1,0:T(8,128)}) %tuple.23, ...), branch_computations={%region_0.0_spmd, %region_1.0_spmd, %region_2.0_spmd, %region_3.0_... | conditional | flops 25770196992 | bytes 73221416 | solution.py:496
  1.5 3.7 %prepare.6 = (s32[24,128]{1,0:T(8,128)S(1)}, s32[24,128]{1,0:T(8,128)S(1)}, s32[24,128]{1,0:T(8,128)S(1)}, s32[24,128]{1,0:T(8,128)S(1)}, bf16[33,128,128]{2,1,0...) custom-call(s32[1]{0:T(128)} %bitcast.4.me_ref, s32[2,256]{1,0:T(2,128)} %get-tuple-element.118.user_ref, ...), custom_call_target="tpu_custom_call" | custom-call | tf_op jit(solution)/shard_map/cond/branch_2_fun/prepare/pallas_call | solution.py:182
  5.2 5.9 %slots.25 = (f32[33,128,128]{2,1,0:T(8,128)S(1)}, f32[520,128]{1,0:T(8,128)S(1)}, f32[520,128]{1,0:T(8,128)S(1)}, f32[520,128]{1,0:T(8,128)S(1)}, f32[520,128]{1,0:T(8,128)S(1)}) custom-call(s32[24,128]{1,0:T(8,128)S(1)} %get-tuple-element.129.table_ref, bf16[2,256,128,128]{3,2,1,0:T(8,128)(2,1)} %get-tuple-element.124.ratings_ref, ...), custom_call_target="tpu_custom_call" | custom-call | flops 6442450944 | bytes 4194304 | tf_op jit(solution)/shard_map/cond/branch_2_fun/slots/pallas_call | solution.py:319
  11.1 3.4 %collective-permute-start.67 = (f32[520,128]{1,0:T(8,128)S(1)}, f32[520,128]{1,0:T(8,128)S(1)}, u32[]{:S(2)}, u32[]{:S(2)}) collective-permute-start(f32[520,128]{1,0:T(8,128)S(1)} %get-tuple-element.141), channel_id=1, source_target_pairs={{0,1},{1,0},{2,3},{3,2},{4,5},{5,4},{6,7},{7,6},{8,9},{9,8},{10,11... | collective-permute-start | bytes 798728 | tf_op jit(solution)/shard_map/cond/branch_2_fun/ppermute | solution.py:431
  14.6 1.7 %collective-permute-start.68 = (f32[520,128]{1,0:T(8,128)S(1)}, f32[520,128]{1,0:T(8,128)S(1)}, u32[]{:S(2)}, u32[]{:S(2)}) collective-permute-start(f32[520,128]{1,0:T(8,128)S(1)} %get-tuple-element.142), channel_id=1, source_target_pairs={{0,2},{1,3},{2,0},{3,1},{4,6},{5,7},{6,4},{7,5},{8,10},{9,11},{10,... | collective-permute-start | bytes 798728 | tf_op jit(solution)/shard_map/cond/branch_2_fun/ppermute | solution.py:431
  16.2 5.1 %slots.24 = (f32[33,128,128]{2,1,0:T(8,128)S(1)}, f32[520,128]{1,0:T(8,128)S(1)}, f32[520,128]{1,0:T(8,128)S(1)}, f32[520,128]{1,0:T(8,128)S(1)}, f32[520,128]{1,0:T(8,128)S(1)}) custom-call(s32[24,128]{1,0:T(8,128)S(1)} %get-tuple-element.123.table_ref, bf16[2,256,128,128]{3,2,1,0:T(8,128)(2,1)} %get-tuple-element.124.ratings_ref, ...), custom_call_target="tpu_custom_call" | custom-call | flops 6442450944 | bytes 4194304 | tf_op jit(solution)/shard_map/cond/branch_2_fun/slots/pallas_call | solution.py:319
  21.4 2.6 %collective-permute-start.60 = (f32[520,128]{1,0:T(8,128)S(1)}, f32[520,128]{1,0:T(8,128)S(1)}, u32[]{:S(2)}, u32[]{:S(2)}) collective-permute-start(f32[520,128]{1,0:T(8,128)S(1)} %get-tuple-element.135), channel_id=1, source_target_pairs={{0,1},{1,0},{2,3},{3,2},{4,5},{5,4},{6,7},{7,6},{8,9},{9,8},{10,11... | collective-permute-start | bytes 798728 | tf_op jit(solution)/shard_map/cond/branch_2_fun/ppermute | solution.py:431
  25.6 2.9 %collective-permute-done.68.refs_2_ = f32[520,128]{1,0:T(8,128)S(1)} collective-permute-done((f32[520,128]{1,0:T(8,128)S(1)}, f32[520,128]{1,0:T(8,128)S(1)}, u32[]{:S(2)}, u32[]{:S(2)}) %collective-permute-start.68) | collective-permute-done | bytes 266272 | tf_op jit(solution)/shard_map/cond/branch_2_fun/ppermute | solution.py:431
  29.2 4.8 %collective-permute-start.70 = (f32[512,128]{1,0:T(8,128)S(1)}, f32[512,128]{1,0:T(8,128)S(1)}, u32[]{:S(2)}, u32[]{:S(2)}) collective-permute-start(f32[512,128]{1,0:T(8,128)S(1)} %items.37), channel_id=1, source_target_pairs={{0,24},{4,28},{8,16},{12,20},{16,8},{20,12},{24,0},{28,4},{1,25},{... | collective-permute-start | bytes 786440 | tf_op jit(solution)/shard_map/cond/branch_2_fun/ppermute | solution.py:431
  34.0 6.6 %collective-permute-done.61.refs_2_ = f32[520,128]{1,0:T(8,128)S(1)} collective-permute-done((f32[520,128]{1,0:T(8,128)S(1)}, f32[520,128]{1,0:T(8,128)S(1)}, u32[]{:S(2)}, u32[]{:S(2)}) %collective-permute-start.61) | collective-permute-done | bytes 266272 | tf_op jit(solution)/shard_map/cond/branch_2_fun/ppermute | solution.py:431
  40.8 4.4 %collective-permute-start.63 = (f32[512,128]{1,0:T(8,128)S(1)}, f32[512,128]{1,0:T(8,128)S(1)}, u32[]{:S(2)}, u32[]{:S(2)}) collective-permute-start(f32[512,128]{1,0:T(8,128)S(1)} %items.36), channel_id=1, source_target_pairs={{0,24},{4,28},{8,16},{12,20},{16,8},{20,12},{24,0},{28,4},{1,25},{... | collective-permute-start | bytes 786440 | tf_op jit(solution)/shard_map/cond/branch_2_fun/ppermute | solution.py:431
  48.6 1.7 %users.12 = (f32[4096,128]{1,0:T(8,128)S(1)}, bf16[33,128,128]{2,1,0:T(8,128)(2,1)S(1)}, bf16[33,128,128]{2,1,0:T(8,128)(2,1)S(1)}) custom-call(s32[24,128]{1,0:T(8,128)S(1)} %get-tuple-element.123.table_ref, f32[4096,128]{1,0:T(8,128)S(1)} %copy-done.2, f32[33,128,128]{2,1,0:T(8,128)S(1)} %get-tuple-element.128.refs_0_, ...), custom_call_target="tpu_custom_call" | custom-call | tf_op jit(solution)/shard_map/cond/branch_2_fun/users/pallas_call | solution.py:364
  56.5 4.4 %collective-permute-done.72.refs_2_ = f32[512,128]{1,0:T(8,128)S(1)} collective-permute-done((f32[512,128]{1,0:T(8,128)S(1)}, f32[512,128]{1,0:T(8,128)S(1)}, u32[]{:S(2)}, u32[]{:S(2)}) %collective-permute-start.72) | collective-permute-done | bytes 262176 | tf_op jit(solution)/shard_map/cond/branch_2_fun/ppermute | solution.py:431
  61.0 5.2 %slots.27 = (f32[33,128,128]{2,1,0:T(8,128)S(1)}, f32[528,128]{1,0:T(8,128)S(1)}, f32[528,128]{1,0:T(8,128)S(1)}, f32[528,128]{1,0:T(8,128)S(1)}, f32[528,128]{1,0:T(8,128)S(1)}) custom-call(s32[24,128]{1,0:T(8,128)S(1)} %get-tuple-element.139.table_ref, bf16[2,256,128,128]{3,2,1,0:T(8,128)(2,1)} %get-tuple-element.124.ratings_ref, ...), custom_call_target="tpu_custom_call" | custom-call | flops 6442450944 | bytes 4194304 | tf_op jit(solution)/shard_map/cond/branch_2_fun/slots/pallas_call | solution.py:319
  66.2 4.0 %collective-permute-start.82 = (f32[528,128]{1,0:T(8,128)S(1)}, f32[528,128]{1,0:T(8,128)S(1)}, u32[]{:S(2)}, u32[]{:S(2)}) collective-permute-start(f32[528,128]{1,0:T(8,128)S(1)} %get-tuple-element.150), channel_id=1, source_target_pairs={{0,2},{1,3},{2,0},{3,1},{4,6},{5,7},{6,4},{7,5},{8,10},{9,11},{10,... | collective-permute-start | bytes 811016 | tf_op jit(solution)/shard_map/cond/branch_2_fun/ppermute | solution.py:431
  70.5 5.3 %slots.26 = (f32[33,128,128]{2,1,0:T(8,128)S(1)}, f32[528,128]{1,0:T(8,128)S(1)}, f32[528,128]{1,0:T(8,128)S(1)}, f32[528,128]{1,0:T(8,128)S(1)}, f32[528,128]{1,0:T(8,128)S(1)}) custom-call(s32[24,128]{1,0:T(8,128)S(1)} %get-tuple-element.122.table_ref, bf16[2,256,128,128]{3,2,1,0:T(8,128)(2,1)} %get-tuple-element.124.ratings_ref, ...), custom_call_target="tpu_custom_call" | custom-call | flops 6442450944 | bytes 4194304 | tf_op jit(solution)/shard_map/cond/branch_2_fun/slots/pallas_call | solution.py:319
  75.8 4.1 %collective-permute-start.74 = (f32[528,128]{1,0:T(8,128)S(1)}, f32[528,128]{1,0:T(8,128)S(1)}, u32[]{:S(2)}, u32[]{:S(2)}) collective-permute-start(f32[528,128]{1,0:T(8,128)S(1)} %get-tuple-element.146), channel_id=1, source_target_pairs={{0,1},{1,0},{2,3},{3,2},{4,5},{5,4},{6,7},{7,6},{8,9},{9,8},{10,11... | collective-permute-start | bytes 811016 | tf_op jit(solution)/shard_map/cond/branch_2_fun/ppermute | solution.py:431
  82.2 5.1 %collective-permute-done.74.refs_1_ = f32[528,128]{1,0:T(8,128)S(1)} collective-permute-done((f32[528,128]{1,0:T(8,128)S(1)}, f32[528,128]{1,0:T(8,128)S(1)}, u32[]{:S(2)}, u32[]{:S(2)}) %collective-permute-start.74) | collective-permute-done | bytes 270368 | tf_op jit(solution)/shard_map/cond/branch_2_fun/ppermute | solution.py:431
  88.8 1.9 %collective-permute-start.79 = (f32[264,128]{1,0:T(8,128)S(1)}, f32[264,128]{1,0:T(8,128)S(1)}, u32[]{:S(2)}, u32[]{:S(2)}) collective-permute-start(f32[264,128]{1,0:T(8,128)S(1)} %slice_add_fusion.10), channel_id=1, source_target_pairs={{0,1},{1,0},{2,3},{3,2},{4,5},{5,4},{6,7},{7,6},{8,9},{9,8},{10,11... | collective-permute-start | bytes 405512 | tf_op jit(solution)/shard_map/cond/branch_2_fun/ppermute | solution.py:431
  91.0 2.2 %collective-permute-start.88 = (f32[256,128]{1,0:T(8,128)S(1)}, f32[256,128]{1,0:T(8,128)S(1)}, u32[]{:S(2)}, u32[]{:S(2)}) collective-permute-start(f32[256,128]{1,0:T(8,128)S(1)} %items.41), channel_id=1, source_target_pairs={{0,2},{1,3},{2,0},{3,1},{4,6},{5,7},{6,4},{7,5},{8,10},{9,11},{10,... | collective-permute-start | bytes 393224 | tf_op jit(solution)/shard_map/cond/branch_2_fun/ppermute | solution.py:431
  93.2 2.5 %collective-permute-start.76 = (f32[256,128]{1,0:T(8,128)S(1)}, f32[256,128]{1,0:T(8,128)S(1)}, u32[]{:S(2)}, u32[]{:S(2)}) collective-permute-start(f32[256,128]{1,0:T(8,128)S(1)} %items.38), channel_id=1, source_target_pairs={{0,2},{1,3},{2,0},{3,1},{4,6},{5,7},{6,4},{7,5},{8,10},{9,11},{10,... | collective-permute-start | bytes 393224 | tf_op jit(solution)/shard_map/cond/branch_2_fun/ppermute | solution.py:431
  99.6 2.4 %collective-permute-start.77 = (f32[512,128]{1,0:T(8,128)S(1)}, f32[512,128]{1,0:T(8,128)S(1)}, u32[]{:S(2)}, u32[]{:S(2)}) collective-permute-start(f32[512,128]{1,0:T(8,128)S(1)} %pad_maximum_fusion.8.refs_0_), channel_id=1, source_target_pairs={{0,1},{1,0},{2,3},{3,2},{4,5},{5,4},{6,7},{7,6},{8,9},{9,8},{10,11... | collective-permute-start | bytes 786440 | tf_op jit(solution)/shard_map/cond/branch_2_fun/ppermute | solution.py:431
  103.0 2.5 %users.13 = f32[4096,128]{1,0:T(8,128)} custom-call(s32[24,128]{1,0:T(8,128)S(1)} %get-tuple-element.122.table_ref, f32[4096,128]{1,0:T(8,128)S(1)} %get-tuple-element.131.rows_ref, f32[33,128,128]{2,1,0:T(8,128)S(1)} %get-tuple-element.138.refs_0_, f32[33,128,128]{2,1,0:T(8,128)S(1)} %get-tuple-element.144.refs_1_), custom_call_target="tpu_custom_call" | custom-call | tf_op jit(solution)/shard_map/cond/branch_2_fun/users/pallas_call | solution.py:364
  107.8 3.3 %collective-permute-done.77.refs_1_ = f32[512,128]{1,0:T(8,128)S(1)} collective-permute-done((f32[512,128]{1,0:T(8,128)S(1)}, f32[512,128]{1,0:T(8,128)S(1)}, u32[]{:S(2)}, u32[]{:S(2)}) %collective-permute-start.77) | collective-permute-done | bytes 262176 | tf_op jit(solution)/shard_map/cond/branch_2_fun/ppermute | solution.py:431
  (65 shorter events, 25.3 us)
Async XLA Ops:
  11.1 14.5 %collective-permute-start.67 = (f32[520,128]{1,0:T(8,128)S(1)}, f32[520,128]{1,0:T(8,128)S(1)}, u32[]{:S(2)}, u32[]{:S(2)}) collective-permute-start(f32[520,128]{1,0:T(8,128)S(1)} %get-tuple-element.141), channel_id=1, source_target_pairs={{0,1},{1,0},{2,3},{3,2},{4,5},{5,4},{6,7},{7,6},{8,9},{9,8},{10,11... | collective-permute-start | bytes 798728 | tf_op jit(solution)/shard_map/cond/branch_2_fun/ppermute | solution.py:431
  14.6 13.9 %collective-permute-start.68 = (f32[520,128]{1,0:T(8,128)S(1)}, f32[520,128]{1,0:T(8,128)S(1)}, u32[]{:S(2)}, u32[]{:S(2)}) collective-permute-start(f32[520,128]{1,0:T(8,128)S(1)} %get-tuple-element.142), channel_id=1, source_target_pairs={{0,2},{1,3},{2,0},{3,1},{4,6},{5,7},{6,4},{7,5},{8,10},{9,11},{10,... | collective-permute-start | bytes 798728 | tf_op jit(solution)/shard_map/cond/branch_2_fun/ppermute | solution.py:431
  16.2 12.9 %collective-permute-start.69 = (f32[520,128]{1,0:T(8,128)S(1)}, f32[520,128]{1,0:T(8,128)S(1)}, u32[]{:S(2)}, u32[]{:S(2)}) collective-permute-start(f32[520,128]{1,0:T(8,128)S(1)} %get-tuple-element.143), channel_id=1, source_target_pairs={{0,3},{1,2},{2,1},{3,0},{4,7},{5,6},{6,5},{7,4},{8,11},{9,10},{10,... | collective-permute-start | bytes 798728 | tf_op jit(solution)/shard_map/cond/branch_2_fun/ppermute | solution.py:431
  21.4 12.7 %collective-permute-start.60 = (f32[520,128]{1,0:T(8,128)S(1)}, f32[520,128]{1,0:T(8,128)S(1)}, u32[]{:S(2)}, u32[]{:S(2)}) collective-permute-start(f32[520,128]{1,0:T(8,128)S(1)} %get-tuple-element.135), channel_id=1, source_target_pairs={{0,1},{1,0},{2,3},{3,2},{4,5},{5,4},{6,7},{7,6},{8,9},{9,8},{10,11... | collective-permute-start | bytes 798728 | tf_op jit(solution)/shard_map/cond/branch_2_fun/ppermute | solution.py:431
  24.0 16.7 %collective-permute-start.61 = (f32[520,128]{1,0:T(8,128)S(1)}, f32[520,128]{1,0:T(8,128)S(1)}, u32[]{:S(2)}, u32[]{:S(2)}) collective-permute-start(f32[520,128]{1,0:T(8,128)S(1)} %get-tuple-element.136), channel_id=1, source_target_pairs={{0,2},{1,3},{2,0},{3,1},{4,6},{5,7},{6,4},{7,5},{8,10},{9,11},{10,... | collective-permute-start | bytes 798728 | tf_op jit(solution)/shard_map/cond/branch_2_fun/ppermute | solution.py:431
  25.6 15.1 %collective-permute-start.62 = (f32[520,128]{1,0:T(8,128)S(1)}, f32[520,128]{1,0:T(8,128)S(1)}, u32[]{:S(2)}, u32[]{:S(2)}) collective-permute-start(f32[520,128]{1,0:T(8,128)S(1)} %get-tuple-element.137), channel_id=1, source_target_pairs={{0,3},{1,2},{2,1},{3,0},{4,7},{5,6},{6,5},{7,4},{8,11},{9,10},{10,... | collective-permute-start | bytes 798728 | tf_op jit(solution)/shard_map/cond/branch_2_fun/ppermute | solution.py:431
  29.2 15.9 %collective-permute-start.70 = (f32[512,128]{1,0:T(8,128)S(1)}, f32[512,128]{1,0:T(8,128)S(1)}, u32[]{:S(2)}, u32[]{:S(2)}) collective-permute-start(f32[512,128]{1,0:T(8,128)S(1)} %items.37), channel_id=1, source_target_pairs={{0,24},{4,28},{8,16},{12,20},{16,8},{20,12},{24,0},{28,4},{1,25},{... | collective-permute-start | bytes 786440 | tf_op jit(solution)/shard_map/cond/branch_2_fun/ppermute | solution.py:431
  40.8 10.3 %collective-permute-start.63 = (f32[512,128]{1,0:T(8,128)S(1)}, f32[512,128]{1,0:T(8,128)S(1)}, u32[]{:S(2)}, u32[]{:S(2)}) collective-permute-start(f32[512,128]{1,0:T(8,128)S(1)} %items.36), channel_id=1, source_target_pairs={{0,24},{4,28},{8,16},{12,20},{16,8},{20,12},{24,0},{28,4},{1,25},{... | collective-permute-start | bytes 786440 | tf_op jit(solution)/shard_map/cond/branch_2_fun/ppermute | solution.py:431
  45.1 10.1 %collective-permute-start.73 = (f32[512,128]{1,0:T(8,128)S(1)}, f32[512,128]{1,0:T(8,128)S(1)}, u32[]{:S(2)}, u32[]{:S(2)}) collective-permute-start(f32[512,128]{1,0:T(8,128)S(1)} %collective-permute-done.70.refs_0_.old_ref), channel_id=1, source_target_pairs={{0,3},{1,2},{2,1},{3,0},{4,7},{5,6},{6,5},{7,4},{8,11},{9,10},{10,... | collective-permute-start | bytes 786440 | tf_op jit(solution)/shard_map/cond/branch_2_fun/ppermute | solution.py:431
  46.4 14.5 %collective-permute-start.72 = (f32[512,128]{1,0:T(8,128)S(1)}, f32[512,128]{1,0:T(8,128)S(1)}, u32[]{:S(2)}, u32[]{:S(2)}) collective-permute-start(f32[512,128]{1,0:T(8,128)S(1)} %collective-permute-done.70.refs_0_.old_ref), channel_id=1, source_target_pairs={{0,2},{1,3},{2,0},{3,1},{4,6},{5,7},{6,4},{7,5},{8,10},{9,11},{10,... | collective-permute-start | bytes 786440 | tf_op jit(solution)/shard_map/cond/branch_2_fun/ppermute | solution.py:431
  47.8 13.1 %collective-permute-start.71 = (f32[512,128]{1,0:T(8,128)S(1)}, f32[512,128]{1,0:T(8,128)S(1)}, u32[]{:S(2)}, u32[]{:S(2)}) collective-permute-start(f32[512,128]{1,0:T(8,128)S(1)} %collective-permute-done.70.refs_0_.old_ref), channel_id=1, source_target_pairs={{0,1},{1,0},{2,3},{3,2},{4,5},{5,4},{6,7},{7,6},{8,9},{9,8},{10,11... | collective-permute-start | bytes 786440 | tf_op jit(solution)/shard_map/cond/branch_2_fun/ppermute | solution.py:431
  51.1 19.4 %collective-permute-start.66 = (f32[512,128]{1,0:T(8,128)S(1)}, f32[512,128]{1,0:T(8,128)S(1)}, u32[]{:S(2)}, u32[]{:S(2)}) collective-permute-start(f32[512,128]{1,0:T(8,128)S(1)} %collective-permute-done.63.refs_0_.old_ref), channel_id=1, source_target_pairs={{0,3},{1,2},{2,1},{3,0},{4,7},{5,6},{6,5},{7,4},{8,11},{9,10},{10,... | collective-permute-start | bytes 786440 | tf_op jit(solution)/shard_map/cond/branch_2_fun/ppermute | solution.py:431
  52.6 17.9 %collective-permute-start.65 = (f32[512,128]{1,0:T(8,128)S(1)}, f32[512,128]{1,0:T(8,128)S(1)}, u32[]{:S(2)}, u32[]{:S(2)}) collective-permute-start(f32[512,128]{1,0:T(8,128)S(1)} %collective-permute-done.63.refs_0_.old_ref), channel_id=1, source_target_pairs={{0,2},{1,3},{2,0},{3,1},{4,6},{5,7},{6,4},{7,5},{8,10},{9,11},{10,... | collective-permute-start | bytes 786440 | tf_op jit(solution)/shard_map/cond/branch_2_fun/ppermute | solution.py:431
  55.3 15.2 %collective-permute-start.64 = (f32[512,128]{1,0:T(8,128)S(1)}, f32[512,128]{1,0:T(8,128)S(1)}, u32[]{:S(2)}, u32[]{:S(2)}) collective-permute-start(f32[512,128]{1,0:T(8,128)S(1)} %collective-permute-done.63.refs_0_.old_ref), channel_id=1, source_target_pairs={{0,1},{1,0},{2,3},{3,2},{4,5},{5,4},{6,7},{7,6},{8,9},{9,8},{10,11... | collective-permute-start | bytes 786440 | tf_op jit(solution)/shard_map/cond/branch_2_fun/ppermute | solution.py:431
  66.2 15.1 %collective-permute-start.82 = (f32[528,128]{1,0:T(8,128)S(1)}, f32[528,128]{1,0:T(8,128)S(1)}, u32[]{:S(2)}, u32[]{:S(2)}) collective-permute-start(f32[528,128]{1,0:T(8,128)S(1)} %get-tuple-element.150), channel_id=1, source_target_pairs={{0,2},{1,3},{2,0},{3,1},{4,6},{5,7},{6,4},{7,5},{8,10},{9,11},{10,... | collective-permute-start | bytes 811016 | tf_op jit(solution)/shard_map/cond/branch_2_fun/ppermute | solution.py:431
  70.2 11.2 %collective-permute-start.86 = (f32[528,128]{1,0:T(8,128)S(1)}, f32[528,128]{1,0:T(8,128)S(1)}, u32[]{:S(2)}, u32[]{:S(2)}) collective-permute-start(f32[528,128]{1,0:T(8,128)S(1)} %get-tuple-element.152), channel_id=1, source_target_pairs={{0,1},{1,0},{2,3},{3,2},{4,5},{5,4},{6,7},{7,6},{8,9},{9,8},{10,11... | collective-permute-start | bytes 811016 | tf_op jit(solution)/shard_map/cond/branch_2_fun/ppermute | solution.py:431
  75.8 11.5 %collective-permute-start.74 = (f32[528,128]{1,0:T(8,128)S(1)}, f32[528,128]{1,0:T(8,128)S(1)}, u32[]{:S(2)}, u32[]{:S(2)}) collective-permute-start(f32[528,128]{1,0:T(8,128)S(1)} %get-tuple-element.146), channel_id=1, source_target_pairs={{0,1},{1,0},{2,3},{3,2},{4,5},{5,4},{6,7},{7,6},{8,9},{9,8},{10,11... | collective-permute-start | bytes 811016 | tf_op jit(solution)/shard_map/cond/branch_2_fun/ppermute | solution.py:431
  79.9 8.8 %collective-permute-start.78 = (f32[528,128]{1,0:T(8,128)S(1)}, f32[528,128]{1,0:T(8,128)S(1)}, u32[]{:S(2)}, u32[]{:S(2)}) collective-permute-start(f32[528,128]{1,0:T(8,128)S(1)} %get-tuple-element.148), channel_id=1, source_target_pairs={{0,2},{1,3},{2,0},{3,1},{4,6},{5,7},{6,4},{7,5},{8,10},{9,11},{10,... | collective-permute-start | bytes 811016 | tf_op jit(solution)/shard_map/cond/branch_2_fun/ppermute | solution.py:431
  81.3 9.4 %collective-permute-start.83 = (f32[264,128]{1,0:T(8,128)S(1)}, f32[264,128]{1,0:T(8,128)S(1)}, u32[]{:S(2)}, u32[]{:S(2)}) collective-permute-start(f32[264,128]{1,0:T(8,128)S(1)} %slice_add_fusion.9), channel_id=1, source_target_pairs={{0,1},{1,0},{2,3},{3,2},{4,5},{5,4},{6,7},{7,6},{8,9},{9,8},{10,11... | collective-permute-start | bytes 405512 | tf_op jit(solution)/shard_map/cond/branch_2_fun/ppermute | solution.py:431
  81.5 9.5 %collective-permute-start.87 = (f32[264,128]{1,0:T(8,128)S(1)}, f32[264,128]{1,0:T(8,128)S(1)}, u32[]{:S(2)}, u32[]{:S(2)}) collective-permute-start(f32[264,128]{1,0:T(8,128)S(1)} %slice_add_fusion.8), channel_id=1, source_target_pairs={{0,2},{1,3},{2,0},{3,1},{4,6},{5,7},{6,4},{7,5},{8,10},{9,11},{10,... | collective-permute-start | bytes 405512 | tf_op jit(solution)/shard_map/cond/branch_2_fun/ppermute | solution.py:431
  97.4 9.3 %collective-permute-start.85 = (f32[512,128]{1,0:T(8,128)S(1)}, f32[512,128]{1,0:T(8,128)S(1)}, u32[]{:S(2)}, u32[]{:S(2)}) collective-permute-start(f32[512,128]{1,0:T(8,128)S(1)} %pad_maximum_fusion.10.refs_4_), channel_id=1, source_target_pairs={{0,2},{1,3},{2,0},{3,1},{4,6},{5,7},{6,4},{7,5},{8,10},{9,11},{10,... | collective-permute-start | bytes 786440 | tf_op jit(solution)/shard_map/cond/branch_2_fun/ppermute | solution.py:431
  97.9 9.9 %collective-permute-start.89 = (f32[512,128]{1,0:T(8,128)S(1)}, f32[512,128]{1,0:T(8,128)S(1)}, u32[]{:S(2)}, u32[]{:S(2)}) collective-permute-start(f32[512,128]{1,0:T(8,128)S(1)} %pad_maximum_fusion.11.refs_6_), channel_id=1, source_target_pairs={{0,1},{1,0},{2,3},{3,2},{4,5},{5,4},{6,7},{7,6},{8,9},{9,8},{10,11... | collective-permute-start | bytes 786440 | tf_op jit(solution)/shard_map/cond/branch_2_fun/ppermute | solution.py:431
  99.6 11.5 %collective-permute-start.77 = (f32[512,128]{1,0:T(8,128)S(1)}, f32[512,128]{1,0:T(8,128)S(1)}, u32[]{:S(2)}, u32[]{:S(2)}) collective-permute-start(f32[512,128]{1,0:T(8,128)S(1)} %pad_maximum_fusion.8.refs_0_), channel_id=1, source_target_pairs={{0,1},{1,0},{2,3},{3,2},{4,5},{5,4},{6,7},{7,6},{8,9},{9,8},{10,11... | collective-permute-start | bytes 786440 | tf_op jit(solution)/shard_map/cond/branch_2_fun/ppermute | solution.py:431
  102.2 8.9 %collective-permute-start.81 = (f32[512,128]{1,0:T(8,128)S(1)}, f32[512,128]{1,0:T(8,128)S(1)}, u32[]{:S(2)}, u32[]{:S(2)}) collective-permute-start(f32[512,128]{1,0:T(8,128)S(1)} %pad_maximum_fusion.9.refs_2_), channel_id=1, source_target_pairs={{0,2},{1,3},{2,0},{3,1},{4,6},{5,7},{6,4},{7,5},{8,10},{9,11},{10,... | collective-permute-start | bytes 786440 | tf_op jit(solution)/shard_map/cond/branch_2_fun/ppermute | solution.py:431
  (9 other events, 81.6 us)
